TPU v7x, 512 devices: a whole 4x4x16 slice. The times are simulated.
512 devices in a mesh: lat: 32 (over z, core), lev: 16 (over x, y).
Axes of the slice: x: 4, y: 4, z: 16, core: 2. Of those that a mesh axis runs over, the one named last changes fastest.
Arguments:
- zonal_velocity: float32 [128, 512, 576], P('lev', 'lat'), may hold values from -6 to 6
- poleward_velocity: float32 [128, 512, 576], P('lev', 'lat'), may hold values from -6 to 6
- thermal_anomaly: float32 [128, 512, 576], P('lev', 'lat'), may hold values from -6 to 6
- scaled_humidity: float32 [128, 512, 576], P('lev', 'lat'), may hold values from 0 to 1
- ground_potential_energy: float32 [512, 576], P('lat'), may hold values from -6 to 6
- layer_depth_factor: float32 [128], replicated, may hold values from 0.02 to 0.2
Outputs:
- carried_heat_anomaly: float32 [128, 512, 576], P('lev', 'lat')
- carried_humidity: float32 [128, 512, 576], P('lev', 'lat')
- revised_zonal_velocity: float32 [128, 512, 576], P('lev', 'lat')
- revised_poleward_velocity: float32 [128, 512, 576], P('lev', 'lat')
- potential_altitude: float32 [128, 512, 576], P('lev', 'lat')
All inputs are finite; a program needn't handle non-finite values.
Results may differ from a plain program's by a relative error of at most 0.00007.
Values sent between devices are 32-bit elements; how exact they have to be, the bound alone decides.
A program may use at most 64 MiB of HBM per device.

v0:
```python
import jax
import jax.numpy as jnp
from jax import lax
from jax.sharding import PartitionSpec as P

ZONAL_RATE = 0.1
MERID_RATE = 0.25
POLAR_CAP = 0.2
MOIST_CORRECTION = 0.6


def with_halo(value, sides, width):
    for axis, dim in sides:
        count, length = (lax.axis_size(axis), value.shape[dim])
        up = [(i, (i + 1) % count) for i in range(count - 1)]
        down = [(j, i) for i, j in up]
        last = lax.slice_in_dim(value, length - width, length, axis=dim)
        initial = lax.slice_in_dim(value, 0, width, axis=dim)
        before = lax.ppermute(last, axis, up)
        after = lax.ppermute(initial, axis, down)
        value = jnp.concatenate([before, value, after], axis=dim)
    return value


def lat_weights(row_index, circle_sum):
    spacing = jnp.pi / circle_sum
    middle_boxes = jnp.cos(-jnp.pi / 2 + (row_index + 0.5) * spacing)
    upper_interface = jnp.where(
        row_index + 1.0 < circle_sum, jnp.cos(-jnp.pi / 2 + (row_index + 1.0) * spacing), 0.0
    )
    lower_interface = jnp.where(row_index > 0.5, jnp.cos(-jnp.pi / 2 + row_index * spacing), 0.0)
    return (middle_boxes[:, None], upper_interface[:, None], lower_interface[:, None])


def transport_scalar(
    tracer,
    tracer_south,
    tracer_north,
    zonal,
    merid,
    poleward_velocity_lower,
    poleward_velocity_upper,
    middle_boxes,
    upper_interface,
    lower_interface,
):
    zonal_coef = ZONAL_RATE / jnp.maximum(middle_boxes, POLAR_CAP)
    east_flux = 0.25 * (zonal + jnp.roll(zonal, -1, 2)) * (tracer + jnp.roll(tracer, -1, 2))
    zonal_div = east_flux - jnp.roll(east_flux, 1, 2)
    north_flux = (
        upper_interface * 0.25 * (merid + poleward_velocity_upper) * (tracer + tracer_north)
    )
    south_flux = (
        lower_interface * 0.25 * (merid + poleward_velocity_lower) * (tracer + tracer_south)
    )
    return tracer - zonal_coef * zonal_div - MERID_RATE / middle_boxes * (north_flux - south_flux)


def update_winds(zonal, merid, potential_altitude, height_south, height_north, middle_boxes):
    zonal_coef = 0.5 * ZONAL_RATE / jnp.maximum(middle_boxes, POLAR_CAP)
    revised_zonal_velocity = zonal - zonal_coef * (
        jnp.roll(potential_altitude, -1, 2) - jnp.roll(potential_altitude, 1, 2)
    )
    revised_poleward_velocity = merid - 0.5 * MERID_RATE * (height_north - height_south)
    return (revised_zonal_velocity, revised_poleward_velocity)


def below_matrix(weights):
    count = weights.shape[0]
    level = jnp.arange(count)
    return jnp.where(level[None, :] >= level[:, None], weights[None, :], 0.0)


def body(
    zonal_velocity,
    poleward_velocity,
    thermal_anomaly,
    scaled_humidity,
    ground_potential_energy,
    layer_depth_factor,
):
    parallel_circles = thermal_anomaly.shape[1]
    first_row = lax.axis_index("lat") * parallel_circles
    circle_sum = parallel_circles * lax.axis_size("lat")
    row_index = (first_row + jnp.arange(parallel_circles)).astype(jnp.float32)
    middle_boxes, upper_interface, lower_interface = lat_weights(row_index, circle_sum)
    bundled_arrays = jnp.stack([thermal_anomaly, scaled_humidity, poleward_velocity])
    padded = with_halo(bundled_arrays, (("lat", 2),), 1)
    south_rows = padded[:, :, :-2]
    north_rows = padded[:, :, 2:]
    carried_heat_anomaly = transport_scalar(
        thermal_anomaly,
        south_rows[0],
        north_rows[0],
        zonal_velocity,
        poleward_velocity,
        south_rows[2],
        north_rows[2],
        middle_boxes,
        upper_interface,
        lower_interface,
    )
    carried_humidity = transport_scalar(
        scaled_humidity,
        south_rows[1],
        north_rows[1],
        zonal_velocity,
        poleward_velocity,
        south_rows[2],
        north_rows[2],
        middle_boxes,
        upper_interface,
        lower_interface,
    )
    density_adjusted_heat = carried_heat_anomaly + MOIST_CORRECTION * carried_humidity
    columns = lax.all_to_all(density_adjusted_heat, "lev", split_axis=2, concat_axis=0, tiled=True)
    level_count = columns.shape[0]
    block_width = columns.shape[2]
    summed = jnp.dot(
        below_matrix(layer_depth_factor),
        columns.reshape(level_count, -1),
        precision=lax.Precision.HIGHEST,
        preferred_element_type=jnp.float32,
    ).reshape(columns.shape)
    ground = lax.dynamic_slice_in_dim(
        ground_potential_energy, lax.axis_index("lev") * block_width, block_width, 1
    )
    column_height = ground[None] + summed
    potential_altitude = lax.all_to_all(
        column_height, "lev", split_axis=0, concat_axis=2, tiled=True
    )
    height_padded = with_halo(potential_altitude, (("lat", 1),), 1)
    revised_zonal_velocity, revised_poleward_velocity = update_winds(
        zonal_velocity,
        poleward_velocity,
        potential_altitude,
        height_padded[:, :-2],
        height_padded[:, 2:],
        middle_boxes,
    )
    return (
        carried_heat_anomaly,
        carried_humidity,
        revised_zonal_velocity,
        revised_poleward_velocity,
        potential_altitude,
    )


def solution(mesh):
    in_specs = (
        P("lev", "lat", None),
        P("lev", "lat", None),
        P("lev", "lat", None),
        P("lev", "lat", None),
        P("lat", None),
        P(),
    )
    out_specs = (
        P("lev", "lat", None),
        P("lev", "lat", None),
        P("lev", "lat", None),
        P("lev", "lat", None),
        P("lev", "lat", None),
    )
    return jax.shard_map(body, mesh=mesh, in_specs=in_specs, out_specs=out_specs, check_vma=False)
```

profile of v0, /device:TPU:225, one launch (start us, length us, event | category | flops | bytes accessed | tf_op | source)
XLA Modules:
  0.0 69.9 jit_solution(6056884697131184158)
XLA Ops:
  0.7 1.5 %pad_maximum_fusion.12 = (f32[3,8,1,576]{3,2,1,0:T(1,128)S(1)}, f32[3,8,1,576]{3,2,1,0:T(1,128)S(1)}) fusion(f32[1,8,16,576]{3,2,1,0:T(8,128)} %bitcast.95, f32[1,8,16,576]{3,2,1,0:T(8,128)} %bitcast.91, f32[1,8,16,576]{3,2,1,0:T(8,128)} %bitcast.93), kind=kLoop, calls=%fused_computation.59 | loop fusion | flops 55296 | bytes 995328 | tf_op jit(solution)/shard_map/slice | solution.py:18
  2.2 5.3 %collective-permute-start.1 = (f32[3,8,1,576]{3,1,2,0:T(8,128)S(1)}, f32[3,8,1,576]{3,1,2,0:T(8,128)S(1)}, u32[]{:S(2)}, u32[]{:S(2)}) collective-permute-start(f32[3,8,1,576]{3,1,2,0:T(8,128)S(1)} %copy.124), channel_id=1, source_target_pairs={{0,16},{16,32},{32,48},{48,64},{64,80},{80,96},{96,112},{112,128},... | collective-permute-start | bytes 165896 | tf_op jit(solution)/shard_map/ppermute | solution.py:19
  7.5 1.9 %collective-permute-start = (f32[3,8,1,576]{3,1,2,0:T(8,128)S(1)}, f32[3,8,1,576]{3,1,2,0:T(8,128)S(1)}, u32[]{:S(2)}, u32[]{:S(2)}) collective-permute-start(f32[3,8,1,576]{3,1,2,0:T(8,128)S(1)} %copy.123), channel_id=1, source_target_pairs={{16,0},{32,16},{48,32},{64,48},{80,64},{96,80},{112,96},{128,112},... | collective-permute-start | bytes 165896 | tf_op jit(solution)/shard_map/ppermute | solution.py:20
  9.4 0.8 %slice.101 = f32[8,16,1]{2,1,0:T(8,128)S(1)} slice(f32[8,16,576]{2,1,0:T(8,128)} %param.8), slice={[0:8], [0:16], [0:1]} | slice | bytes 1024 | tf_op jit(solution)/shard_map/jit(_roll_static)/slice | solution.py:48
  10.3 1.1 %slice.100 = f32[8,16,575]{2,1,0:T(8,128)S(1)} slice(f32[8,16,576]{2,1,0:T(8,128)} %param.8), slice={[0:8], [0:16], [1:576]} | slice | bytes 588800 | tf_op jit(solution)/shard_map/jit(_roll_static)/slice | solution.py:48
  12.3 2.0 %collective-permute-done = f32[3,8,1,576]{3,1,2,0:T(8,128)S(1)} collective-permute-done((f32[3,8,1,576]{3,1,2,0:T(8,128)S(1)}, f32[3,8,1,576]{3,1,2,0:T(8,128)S(1)}, u32[]{:S(2)}, u32[]{:S(2)}) %collective-permute-start) | collective-permute-done | bytes 55328 | tf_op jit(solution)/shard_map/ppermute | solution.py:20
  14.3 1.4 %multiply_add_fusion = (f32[8,16,576]{2,1,0:T(8,128)S(1)}, f32[8,16,576]{2,1,0:T(8,128)}, f32[8,16,576]{2,1,0:T(8,128)}) fusion(f32[8,16,576]{2,1,0:T(8,128)S(1)} %copy-done.1, f32[1,8,16,576]{3,2,1,0:T(8,128)S(1)} %bitcast.96, f32[1,8,16,576]{3,2,1,0:T(8,128)S(1)} %bitcast.92, f32[1,8,16,576]{3,2,1,0:T(8,128)S(1)} %bitcast.94, ...), kind=kLoop, calls=%fused_computation.53 | loop fusion | flops 3391488 | bytes 3944704 | tf_op jit(solution)/shard_map/add | solution.py:115
  15.8 0.8 %copy.118 = f32[8,16,576]{1,0,2:T(8,128)S(1)} copy(f32[8,16,576]{2,1,0:T(8,128)S(1)} %get-tuple-element.20) | data formatting | bytes 589824 | tf_op jit(solution)/shard_map/add | solution.py:115
  16.6 1.6 %reshape.65 = f32[16,1,4608]{2,1,0:T(1,128)} reshape(f32[576,8,16]{2,1,0:T(8,128)S(1)} %bitcast.89) | data formatting | bytes 589824
  18.2 6.8 %all-to-all-start = ((f32[16,1,4608]{2,1,0:T(1,128)}), f32[16,1,4608]{2,1,0:T(1,128)S(1)}, u32[]{:S(2)}, u32[]{:S(2)}) async-start(f32[16,1,4608]{2,1,0:T(1,128)} %reshape.65), calls=%async_computation | async-start | bytes 589824 | tf_op jit(solution)/shard_map/all_to_all | solution.py:116
  25.0 7.4 %all-to-all-done = f32[16,1,4608]{2,1,0:T(1,128)S(1)} async-done(((f32[16,1,4608]{2,1,0:T(1,128)}), f32[16,1,4608]{2,1,0:T(1,128)S(1)}, u32[]{:S(2)}, u32[]{:S(2)}) %all-to-all-start) | async-done | bytes 294944 | tf_op jit(solution)/shard_map/all_to_all | solution.py:116
  33.0 1.4 %reduce = f32[16,4608]{1,0:T(8,128)S(1)} reduce(f32[16,1,4608]{2,1,0:T(1,128)S(1)} %all-to-all-done, f32[]{:T(128)} %broadcast.227), dimensions={1}, to_apply=%all_to_all.24.reduce_sub_computation | reduce | bytes 589828 | tf_op jit(solution)/shard_map/all_to_all | solution.py:116
  35.1 2.0 %copy.119 = f32[8,16,16,36]{3,1,0,2:T(8,128)} copy(f32[8,16,16,36]{1,0,3,2:T(8,128)S(1)} %bitcast.90) | data formatting | bytes 589824 | tf_op jit(solution)/shard_map/all_to_all | solution.py:116
  37.1 1.7 %reshape.63 = f32[128,576]{1,0:T(8,128)S(1)} reshape(f32[16,8,16,36]{3,2,1,0:T(8,128)} %bitcast.97) | data formatting | bytes 589824 | tf_op jit(solution)/shard_map/reshape | solution.py:121
  39.9 2.0 %reshape.67 = f32[16,1,4608]{2,1,0:T(1,128)} reshape(f32[128,16,36]{2,1,0:T(8,128)S(1)} %copy.121) | data formatting | bytes 589824
  41.9 3.5 %all-to-all-start.1 = ((f32[16,1,4608]{2,1,0:T(1,128)}), f32[16,1,4608]{2,1,0:T(1,128)S(1)}, u32[]{:S(2)}, u32[]{:S(2)}) async-start(f32[16,1,4608]{2,1,0:T(1,128)} %reshape.67), calls=%async_computation.1 | async-start | bytes 589824 | tf_op jit(solution)/shard_map/all_to_all | solution.py:129
  45.5 8.1 %all-to-all-done.1 = f32[16,1,4608]{2,1,0:T(1,128)S(1)} async-done(((f32[16,1,4608]{2,1,0:T(1,128)}), f32[16,1,4608]{2,1,0:T(1,128)S(1)}, u32[]{:S(2)}, u32[]{:S(2)}) %all-to-all-start.1) | async-done | bytes 294944 | tf_op jit(solution)/shard_map/all_to_all | solution.py:129
  53.6 1.4 %reduce.1 = f32[16,4608]{1,0:T(8,128)S(1)} reduce(f32[16,1,4608]{2,1,0:T(1,128)S(1)} %all-to-all-done.1, f32[]{:T(128)} %broadcast.227), dimensions={1}, to_apply=%all_to_all.27.reduce_sub_computation | reduce | bytes 589828 | tf_op jit(solution)/shard_map/all_to_all | solution.py:129
  55.0 1.3 %reshape.68 = f32[128,16,36]{2,1,0:T(8,128)S(1)} reshape(f32[16,4608]{1,0:T(8,128)S(1)} %reduce.1) | data formatting | bytes 589824
  57.7 5.0 %collective-permute-start.3 = (f32[8,1,576]{2,1,0:T(1,128)S(1)}, f32[8,1,576]{2,1,0:T(1,128)S(1)}, u32[]{:S(2)}, u32[]{:S(2)}) collective-permute-start(f32[8,1,576]{2,1,0:T(1,128)S(1)} %get-tuple-element.28), channel_id=1, source_target_pairs={{0,16},{16,32},{32,48},{48,64},{64,80},{80,96},{96,112},{112,128},... | collective-permute-start | bytes 55304 | tf_op jit(solution)/shard_map/ppermute | solution.py:19
  62.7 1.9 %collective-permute-start.2 = (f32[8,1,576]{2,1,0:T(1,128)S(1)}, f32[8,1,576]{2,1,0:T(1,128)S(1)}, u32[]{:S(2)}, u32[]{:S(2)}) collective-permute-start(f32[8,1,576]{2,1,0:T(1,128)S(1)} %get-tuple-element.27), channel_id=1, source_target_pairs={{16,0},{32,16},{48,32},{64,48},{80,64},{96,80},{112,96},{128,112},... | collective-permute-start | bytes 55304 | tf_op jit(solution)/shard_map/ppermute | solution.py:20
  64.6 0.9 %fusion.31 = f32[8,16,576]{2,1,0:T(8,128)} fusion(f32[8,16,576]{2,1,0:T(8,128)S(1)} %copy-done.5, f32[8,16,1]{2,1,0:T(8,128)S(1)} %get-tuple-element.30, f32[8,16,575]{2,1,0:T(8,128)S(1)} %get-tuple-element.32, f32[8,16,575]{2,1,0:T(8,128)S(1)} %get-tuple-element.31, f32[8,16,1]{2,1,0:T(8,128)S(1)} %get-tuple-element.29, f32[16]{0:T(128)S(1)} %maximum_divide_fusion), kind=kLoop, calls=%fused_computation.52 | loop fusion | flops 368640 | bytes 1179712 | tf_op jit(solution)/shard_map/sub | solution.py:61
  65.5 3.5 %collective-permute-done.2 = f32[8,1,576]{2,1,0:T(1,128)S(1)} collective-permute-done((f32[8,1,576]{2,1,0:T(1,128)S(1)}, f32[8,1,576]{2,1,0:T(1,128)S(1)}, u32[]{:S(2)}, u32[]{:S(2)}) %collective-permute-start.2) | collective-permute-done | bytes 18464 | tf_op jit(solution)/shard_map/ppermute | solution.py:20
  69.0 0.8 %fusion.2 = f32[8,16,576]{2,1,0:T(8,128)} fusion(f32[8,16,576]{2,1,0:T(8,128)S(1)} %copy-done.4, f32[8,16,576]{2,1,0:T(8,128)S(1)} %all_to_all.30, f32[8,1,576]{2,1,0:T(1,128)S(1)} %collective-permute-done.3, f32[8,1,576]{2,1,0:T(1,128)S(1)} %collective-permute-done.2), kind=kLoop, calls=%fused_computation.4 | loop fusion | flops 368640 | bytes 921600 | tf_op jit(solution)/shard_map/sub | solution.py:64
  (43 shorter events, 4.9 us)
Async XLA Ops:
  0.6 24.3 %copy-start = (f32[16,576]{1,0:T(8,128)S(1)}, f32[16,576]{1,0:T(8,128)}, u32[]{:S(2)}) copy-start(f32[16,576]{1,0:T(8,128)} %param.10) | copy-start | bytes 110596
  0.6 10.9 %copy-start.1 = (f32[8,16,576]{2,1,0:T(8,128)S(1)}, f32[8,16,576]{2,1,0:T(8,128)}, u32[]{:S(2)}) copy-start(f32[8,16,576]{2,1,0:T(8,128)} %param.9) | copy-start | bytes 884740
  0.7 11.2 %copy-start.2 = (f32[8,16,576]{2,1,0:T(8,128)S(1)}, f32[8,16,576]{2,1,0:T(8,128)}, u32[]{:S(2)}) copy-start(f32[8,16,576]{2,1,0:T(8,128)} %param.8) | copy-start | bytes 884740
  0.7 10.7 %copy-start.5 = (f32[8,16,576]{2,1,0:T(8,128)S(1)}, f32[8,16,576]{2,1,0:T(8,128)}, u32[]{:S(2)}) copy-start(f32[8,16,576]{2,1,0:T(8,128)} %param.6) | copy-start | bytes 884740
  0.7 11.2 %slice-start = ((f32[8,16,576]{2,1,0:T(8,128)}), f32[8,16,1]{2,1,0:T(8,128)S(1)}, s32[]{:S(2)}) async-start(f32[8,16,576]{2,1,0:T(8,128)} %param.6), calls=%async_computation.2 | async-start | bytes 131072 | tf_op jit(solution)/shard_map/jit(_roll_static)/slice | solution.py:48
  2.2 10.1 %collective-permute-start.1 = (f32[3,8,1,576]{3,1,2,0:T(8,128)S(1)}, f32[3,8,1,576]{3,1,2,0:T(8,128)S(1)}, u32[]{:S(2)}, u32[]{:S(2)}) collective-permute-start(f32[3,8,1,576]{3,1,2,0:T(8,128)S(1)} %copy.124), channel_id=1, source_target_pairs={{0,16},{16,32},{32,48},{48,64},{64,80},{80,96},{96,112},{112,128},... | collective-permute-start | bytes 165896 | tf_op jit(solution)/shard_map/ppermute | solution.py:19
  7.5 6.8 %collective-permute-start = (f32[3,8,1,576]{3,1,2,0:T(8,128)S(1)}, f32[3,8,1,576]{3,1,2,0:T(8,128)S(1)}, u32[]{:S(2)}, u32[]{:S(2)}) collective-permute-start(f32[3,8,1,576]{3,1,2,0:T(8,128)S(1)} %copy.123), channel_id=1, source_target_pairs={{16,0},{32,16},{48,32},{64,48},{80,64},{96,80},{112,96},{128,112},... | collective-permute-start | bytes 165896 | tf_op jit(solution)/shard_map/ppermute | solution.py:20
  11.4 2.9 %copy-start.4 = (f32[8,16,576]{2,1,0:T(8,128)S(1)}, f32[8,16,576]{2,1,0:T(8,128)}, u32[]{:S(2)}) copy-start(f32[8,16,576]{2,1,0:T(8,128)} %param.7) | copy-start | bytes 884740
  18.2 14.3 %all-to-all-start = ((f32[16,1,4608]{2,1,0:T(1,128)}), f32[16,1,4608]{2,1,0:T(1,128)S(1)}, u32[]{:S(2)}, u32[]{:S(2)}) async-start(f32[16,1,4608]{2,1,0:T(1,128)} %reshape.65), calls=%async_computation | async-start | bytes 589824 | tf_op jit(solution)/shard_map/all_to_all | solution.py:116
  35.1 3.8 %copy-start.6 = (f32[128]{0:T(128)S(1)}, f32[128]{0:T(128)}, u32[]{:S(2)}) copy-start(f32[128]{0:T(128)} %param.11) | copy-start | bytes 1540
  41.9 11.7 %all-to-all-start.1 = ((f32[16,1,4608]{2,1,0:T(1,128)}), f32[16,1,4608]{2,1,0:T(1,128)S(1)}, u32[]{:S(2)}, u32[]{:S(2)}) async-start(f32[16,1,4608]{2,1,0:T(1,128)} %reshape.67), calls=%async_computation.1 | async-start | bytes 589824 | tf_op jit(solution)/shard_map/all_to_all | solution.py:129
  57.4 12.4 %copy-start.3 = (f32[8,16,576]{2,1,0:T(8,128)}, f32[8,16,576]{2,1,0:T(8,128)S(1)}, u32[]{:S(2)}) copy-start(f32[8,16,576]{2,1,0:T(8,128)S(1)} %all_to_all.30) | copy-start | bytes 884740
  57.7 7.8 %collective-permute-start.3 = (f32[8,1,576]{2,1,0:T(1,128)S(1)}, f32[8,1,576]{2,1,0:T(1,128)S(1)}, u32[]{:S(2)}, u32[]{:S(2)}) collective-permute-start(f32[8,1,576]{2,1,0:T(1,128)S(1)} %get-tuple-element.28), channel_id=1, source_target_pairs={{0,16},{16,32},{32,48},{48,64},{64,80},{80,96},{96,112},{112,128},... | collective-permute-start | bytes 55304 | tf_op jit(solution)/shard_map/ppermute | solution.py:19
  62.7 6.3 %collective-permute-start.2 = (f32[8,1,576]{2,1,0:T(1,128)S(1)}, f32[8,1,576]{2,1,0:T(1,128)S(1)}, u32[]{:S(2)}, u32[]{:S(2)}) collective-permute-start(f32[8,1,576]{2,1,0:T(1,128)S(1)} %get-tuple-element.27), channel_id=1, source_target_pairs={{16,0},{32,16},{48,32},{64,48},{80,64},{96,80},{112,96},{128,112},... | collective-permute-start | bytes 55304 | tf_op jit(solution)/shard_map/ppermute | solution.py:20
where the time goes:
time: 70.6 us; the launch traced here: 69.9 us
  starting transfers between devices  24.4 us (35%)
  waiting for transfers between devices  21 us (30%)
  local copies, waits for them, and re-layouts  15.4 us (22%)
  other arithmetic  7.65 us (11%)
  between operations  0.97 us (1%)
    ppermute x2, starting transfers between devices, with_halo(): before = lax.ppermute(last, axis, up)  10.3 us
    all_to_all x1, waiting for transfers between devices, body(): lax.all_to_all(column_height, 'lev', split_axis=0, concat_axis=2, tiled=T...  8.11 us
    all_to_all x1, waiting for transfers between devices, body(): lax.all_to_all(density_adjusted_heat, 'lev', split_axis=2, concat_axis=0,...  7.43 us
    all_to_all x1, starting transfers between devices, body(): lax.all_to_all(density_adjusted_heat, 'lev', split_axis=2, concat_axis=0,...  6.75 us
    unnamed x20, local copies, waits for them, and re-layouts  5.72 us
    ppermute x2, waiting for transfers between devices, with_halo(): after = lax.ppermute(initial, axis, down)  5.43 us
    ppermute x2, starting transfers between devices, with_halo(): after = lax.ppermute(initial, axis, down)  3.84 us
    all_to_all x1, starting transfers between devices, body(): lax.all_to_all(column_height, 'lev', split_axis=0, concat_axis=2, tiled=T...  3.54 us
  transfers between devices with their start and end apart: 6, of which 4 were waited for; matrix products, arithmetic and copies ran while one was open for 5% of the time, Pallas kernels for 0%

commit v1 on v0

v1 whole, which is shorter than its diff:
```python
import functools
import jax
import jax.numpy as jnp
from jax import lax
from jax.experimental import pallas as pl
from jax.experimental.pallas import tpu as pltpu
from jax.sharding import PartitionSpec as P

ZONAL_RATE = 0.1
MERID_RATE = 0.25
POLAR_CAP = 0.2
MOIST_CORRECTION = 0.6
F32 = jnp.float32
MESH = pl.DeviceIdType.MESH


def lat_weights(row_index, circle_sum):
    spacing = jnp.pi / circle_sum
    middle_boxes = jnp.cos(-jnp.pi / 2 + (row_index + 0.5) * spacing)
    upper_interface = jnp.where(
        row_index + 1.0 < circle_sum, jnp.cos(-jnp.pi / 2 + (row_index + 1.0) * spacing), 0.0
    )
    lower_interface = jnp.where(row_index > 0.5, jnp.cos(-jnp.pi / 2 + row_index * spacing), 0.0)
    return middle_boxes, upper_interface, lower_interface


def widen(column, width):
    whole, rest = width // 128, width % 128
    parts = [column] * whole + ([column[:, :rest]] if rest else [])
    return jnp.concatenate(parts, axis=1)


def wrapped(value):
    width = value.shape[1]
    extra = -width % 128
    if extra == 0:
        return value
    return jnp.concatenate([value, value[:, :extra]], axis=1)


def east(full):
    return pltpu.roll(full, full.shape[1] - 1, 1)


def west(full, width):
    size = full.shape[1]
    rolled = pltpu.roll(full, 1, 1)
    if size == width:
        return rolled
    last = pltpu.roll(full[:, size - 128 :], 128 - (width - 1 - (size - 128)), 1)
    lane = lax.broadcasted_iota(jnp.int32, last.shape, 1)
    start = jnp.where(lane == 0, last, rolled[:, :128])
    return jnp.concatenate([start, rolled[:, 128:]], axis=1)


def advect_kernel(
    u_hbm, v_hbm, t_hbm, q_hbm, g_hbm, w_hbm,
    t_out, q_out, u_out, v_out, c_out, b_out,
    u_ref, v_ref, t_ref, q_ref, g_ref, w_ref,
    raw_send, raw_recv, part_send, part_recv,
    early_send, early_recv, late_send, late_recv, flux_ref, edge_ref,
    in_sem, raw_ssem, raw_rsem, part_ssem, part_rsem,
    early_ssem, early_rsem, late_ssem, late_rsem,
):
    lat, lev = lax.axis_index("lat"), lax.axis_index("lev")
    lats, levs = lax.axis_size("lat"), lax.axis_size("lev")
    levels, rows, width = t_ref.shape
    circle_sum = rows * lats
    full = width + (-width % 128)
    has_south, has_north = lat > 0, lat < lats - 1

    barrier = pltpu.get_barrier_semaphore()

    @pl.when(has_south)
    def _():
        pl.semaphore_signal(barrier, inc=1, device_id=(lat - 1, lev), device_id_type=MESH)

    @pl.when(has_north)
    def _():
        pl.semaphore_signal(barrier, inc=1, device_id=(lat + 1, lev), device_id_type=MESH)

    def greet(step, carry):
        pl.semaphore_signal(barrier, inc=1, device_id=(lat, lev + 1 + step), device_id_type=MESH)
        return carry

    lax.fori_loop(0, levs - 1 - lev, greet, 0)

    loads = [
        pltpu.make_async_copy(source, target, in_sem.at[n])
        for n, (source, target) in enumerate(
            [(t_hbm, t_ref), (q_hbm, q_ref), (v_hbm, v_ref), (u_hbm, u_ref), (g_hbm, g_ref), (w_hbm, w_ref)]
        )
    ]
    for load in loads:
        load.start()

    band = (lat * rows + lax.broadcasted_iota(jnp.int32, (rows, 128), 0)).astype(F32)
    centre, upper, lower = lat_weights(band, circle_sum)
    zonal = ZONAL_RATE / jnp.maximum(centre, POLAR_CAP)
    merid = MERID_RATE / centre
    beside = lat * rows - 1 + (rows + 1) * lax.broadcasted_iota(jnp.int32, (8, 128), 0)
    beside_centre, _, _ = lat_weights(beside.astype(F32), circle_sum)
    merid_beside = MERID_RATE / beside_centre
    south_interface, north_interface = lower[0:1], upper[rows - 1 :]
    merid_south, merid_north = merid_beside[0:1], merid_beside[1:2]
    row_of = lax.broadcasted_iota(jnp.int32, (rows, width), 0)
    upper_wide = widen(upper, width)
    zonal_wide, merid_wide = widen(zonal, width), widen(merid, width)

    def packed(ref, row):
        return ref[:, row, :]

    def spread(row):
        return widen(jnp.broadcast_to(row, (levels, 128)), width)

    if lats > 1:
        @pl.when(jnp.logical_not(has_north))
        def _():
            raw_recv[0] = jnp.zeros(raw_recv.shape[1:], F32)
            part_recv[0] = jnp.zeros(part_recv.shape[1:], F32)

        @pl.when(jnp.logical_not(has_south))
        def _():
            raw_recv[1] = jnp.zeros(raw_recv.shape[1:], F32)
            part_recv[1] = jnp.zeros(part_recv.shape[1:], F32)

    for load in loads[:3]:
        load.wait()

    for side, row in ((0, 0), (1, rows - 1)):
        raw_send[side, 0] = packed(v_ref, row)
        raw_send[side, 1] = packed(t_ref, row)
        raw_send[side, 2] = packed(q_ref, row)
    pl.semaphore_wait(
        barrier, lev + has_south.astype(jnp.int32) + has_north.astype(jnp.int32)
    )

    def halo(send, recv, ssem, rsem, side):
        return pltpu.make_async_remote_copy(
            src_ref=send.at[side],
            dst_ref=recv.at[side],
            send_sem=ssem.at[side],
            recv_sem=rsem.at[side],
            device_id=(lat - 1 if side == 0 else lat + 1, lev),
            device_id_type=MESH,
        )

    raw_copies = [halo(raw_send, raw_recv, raw_ssem, raw_rsem, side) for side in (0, 1)]
    part_copies = [halo(part_send, part_recv, part_ssem, part_rsem, side) for side in (0, 1)]
    pl.when(has_south)(raw_copies[0].start)
    pl.when(has_north)(raw_copies[1].start)

    for load in loads[3:]:
        load.wait()

    for side, row, inner, interface, sign in (
        (0, 0, 1, upper[0:1], -1.0),
        (1, rows - 1, rows - 2, lower[rows - 1 :], 1.0),
    ):
        tracer = raw_send[side, 1] + MOIST_CORRECTION * raw_send[side, 2]
        tracer_in = packed(t_ref, inner) + MOIST_CORRECTION * packed(q_ref, inner)
        wind_in = packed(v_ref, inner)
        flux_in = spread(interface * 0.25) * (raw_send[side, 0] + wind_in) * (tracer + tracer_in)
        wind = wrapped(packed(u_ref, row))
        around = wrapped(tracer)
        flux = 0.25 * (wind + east(wind)) * (around + east(around))
        change = (flux - west(flux, width))[:, :width]
        part_send[side, 0] = (
            tracer
            - spread(zonal[row : row + 1]) * change
            + sign * spread(merid[row : row + 1]) * flux_in
        )
        part_send[side, 1] = jnp.broadcast_to(g_ref[row : row + 1, :], (levels, width))
    pl.when(has_south)(part_copies[0].start)
    pl.when(has_north)(part_copies[1].start)

    def partial(k, carry):
        zonal_sum, merid_sum, own_sum = carry
        weight = w_ref[lev * levels + k]
        tracer = t_ref[k] + MOIST_CORRECTION * q_ref[k]
        around = wrapped(tracer)
        wind = wrapped(u_ref[k])
        zonal_sum += weight * ((wind + east(wind)) * (around + east(around)))
        cross = v_ref[k]
        merid_sum += weight * (
            (cross + pltpu.roll(cross, rows - 1, 0)) * (tracer + pltpu.roll(tracer, rows - 1, 0))
        )
        return zonal_sum, merid_sum, own_sum + weight * tracer

    zonal_sum, merid_sum, own_sum = lax.fori_loop(
        0,
        levels,
        partial,
        (jnp.zeros((rows, full), F32), jnp.zeros((rows, width), F32), jnp.zeros((rows, width), F32)),
    )
    north_sum = jnp.where(row_of < rows - 1, 0.25 * upper_wide * merid_sum, 0.0)
    early_send[...] = (
        own_sum
        - zonal_wide * (0.25 * (zonal_sum - west(zonal_sum, width)))[:, :width]
        - merid_wide * (north_sum - pltpu.roll(north_sum, 1, 0))
    )

    def exchange(send, recv, ssem, rsem, other):
        return pltpu.make_async_remote_copy(
            src_ref=send,
            dst_ref=recv.at[lev],
            send_sem=ssem.at[other],
            recv_sem=rsem.at[lev],
            device_id=(lat, other),
            device_id_type=MESH,
        )

    def send_early(other, carry):
        exchange(early_send, early_recv, early_ssem, early_rsem, other).start()
        return carry

    lax.fori_loop(0, lev, send_early, 0)

    pl.when(has_south)(raw_copies[1].wait_recv)
    pl.when(has_north)(raw_copies[0].wait_recv)
    for side, interface in ((0, north_interface), (1, south_interface)):
        mine = 1 - side
        wind = spread(interface * 0.25) * (raw_send[mine, 0] + raw_recv[side, 0])
        flux_ref[side, 0] = wind * (raw_send[mine, 1] + raw_recv[side, 1])
        flux_ref[side, 1] = wind * (raw_send[mine, 2] + raw_recv[side, 2])
    level_of = lax.broadcasted_iota(jnp.int32, (levels, 128), 0)
    weights = jnp.zeros((levels, 128), F32)
    for k in range(levels):
        weights = jnp.where(level_of == k, w_ref[lev * levels + k], weights)
    weights = widen(weights, width)
    pl.when(has_south)(part_copies[1].wait_recv)
    pl.when(has_north)(part_copies[0].wait_recv)
    for side, exists, merid_edge, sign in (
        (0, has_north, merid_north, 1.0),
        (1, has_south, merid_south, -1.0),
    ):
        flux = flux_ref[side, 0] + MOIST_CORRECTION * flux_ref[side, 1]
        part = part_recv[side, 0]
        late_send[side : side + 1] = jnp.sum(weights * flux, axis=0, keepdims=True)
        late_send[side + 2 : side + 3] = jnp.sum(weights * part, axis=0, keepdims=True)
        beyond = weights * (part + sign * spread(merid_edge) * flux)
        edge_ref[side] = jnp.where(exists, beyond, 0.0)

    def send_late(other, carry):
        exchange(late_send, late_recv, late_ssem, late_rsem, other).start()
        return carry

    lax.fori_loop(0, lev, send_late, 0)

    half_zonal = 0.5 * zonal_wide

    def local(step, carry):
        below, below_north, below_south = carry
        k = levels - 1 - step
        weight = w_ref[lev * levels + k]
        wind, cross = u_ref[k], v_ref[k]
        wind_full = wrapped(wind)
        wind_pair = 0.25 * (wind_full + east(wind_full))
        cross_pair = 0.25 * upper_wide * (cross + pltpu.roll(cross, rows - 1, 0))

        def moved(tracer, kind):
            around = wrapped(tracer)
            flux = wind_pair * (around + east(around))
            change = (flux - west(flux, width))[:, :width]
            inner = cross_pair * (tracer + pltpu.roll(tracer, rows - 1, 0))
            north = jnp.where(row_of == rows - 1, flux_ref[0, kind, pl.ds(k, 1), :], inner)
            south = jnp.where(row_of == 0, flux_ref[1, kind, pl.ds(k, 1), :], pltpu.roll(inner, 1, 0))
            return tracer - zonal_wide * change - merid_wide * (north - south)

        heat, humid = moved(t_ref[k], 0), moved(q_ref[k], 1)
        t_out[k] = heat
        q_out[k] = humid
        below = below + weight * (heat + MOIST_CORRECTION * humid)
        below_north = below_north + edge_ref[0, pl.ds(k, 1), :]
        below_south = below_south + edge_ref[1, pl.ds(k, 1), :]
        c_out[k] = below
        around = wrapped(below)
        u_out[k] = wind - half_zonal * (east(around) - west(around, width))[:, :width]
        north = jnp.where(row_of == rows - 1, below_north, pltpu.roll(below, rows - 1, 0))
        south = jnp.where(row_of == 0, below_south, pltpu.roll(below, 1, 0))
        v_out[k] = cross - 0.5 * MERID_RATE * (north - south)
        return below, below_north, below_south

    lax.fori_loop(
        0,
        levels,
        local,
        (jnp.zeros((rows, width), F32), jnp.zeros((1, width), F32), jnp.zeros((1, width), F32)),
    )

    def add_early(other, total):
        pltpu.make_async_copy(early_recv.at[other], early_recv.at[other], early_rsem.at[other]).wait()
        return total + early_recv[other]

    def add_late(other, total):
        pltpu.make_async_copy(late_recv.at[other], late_recv.at[other], late_rsem.at[other]).wait()
        return total + late_recv[other]

    total = lax.fori_loop(lev + 1, levs, add_early, g_ref[...])
    edges = lax.fori_loop(lev + 1, levs, add_late, jnp.zeros(late_send.shape, F32))
    north_flux, south_flux = edges[0:1], edges[1:2]
    total = total + merid_wide * (
        jnp.where(row_of == 0, south_flux, 0.0) - jnp.where(row_of == rows - 1, north_flux, 0.0)
    )
    beyond_north = part_recv[0, 1, 0:1] + edges[2:3] + widen(merid_north, width) * north_flux
    beyond_south = part_recv[1, 1, 0:1] + edges[3:4] - widen(merid_south, width) * south_flux
    beyond_north = jnp.where(has_north, beyond_north, 0.0)
    beyond_south = jnp.where(has_south, beyond_south, 0.0)
    around = wrapped(total)
    b_out[0] = total
    b_out[1] = half_zonal * (east(around) - west(around, width))[:, :width]
    north = jnp.where(row_of == rows - 1, beyond_north, pltpu.roll(total, rows - 1, 0))
    south = jnp.where(row_of == 0, beyond_south, pltpu.roll(total, 1, 0))
    b_out[2] = 0.5 * MERID_RATE * (north - south)

    for side, exists in ((0, has_south), (1, has_north)):
        pl.when(exists)(raw_copies[side].wait_send)
        pl.when(exists)(part_copies[side].wait_send)

    def sent(other, carry):
        exchange(early_send, early_recv, early_ssem, early_rsem, other).wait_send()
        exchange(late_send, late_recv, late_ssem, late_rsem, other).wait_send()
        return carry

    lax.fori_loop(0, lev, sent, 0)


def finish_kernel(t_in, q_in, u_in, v_in, c_in, b_in, t, q, u, v, h, u_new, v_new, h_new, sems):
    copies = [
        pltpu.make_async_copy(source, target, sems.at[n])
        for n, (source, target) in enumerate([(t_in, t), (q_in, q), (h_new, h), (u_new, u), (v_new, v)])
    ]
    copies[0].start()
    copies[1].start()
    for k in range(t_in.shape[0]):
        h_new[k] = c_in[k] + b_in[0]
    copies[2].start()
    for k in range(t_in.shape[0]):
        u_new[k] = u_in[k] - b_in[1]
    copies[3].start()
    for k in range(t_in.shape[0]):
        v_new[k] = v_in[k] - b_in[2]
    copies[4].start()
    for copy in copies:
        copy.wait()


def body(zonal, poleward, heat, humidity, ground, weights):
    levels, rows, width = heat.shape
    levs = lax.axis_size("lev")
    slab = (levels, rows, width)
    anywhere = pl.BlockSpec(memory_space=pl.ANY)
    vmem = pl.BlockSpec(memory_space=pltpu.VMEM)
    dma = pltpu.SemaphoreType.DMA
    args = [pltpu.with_memory_space_constraint(x, pltpu.HBM) for x in (zonal, poleward, heat, humidity, ground, weights)]
    parts = pl.pallas_call(
        advect_kernel,
        name="advect",
        out_shape=[pltpu.VMEM(slab, F32)] * 5 + [pltpu.VMEM((3, rows, width), F32)],
        in_specs=[anywhere] * 6,
        out_specs=[vmem] * 6,
        scratch_shapes=[pltpu.VMEM(slab, F32)] * 4
        + [
            pltpu.VMEM((rows, width), F32),
            pltpu.SMEM(weights.shape, F32),
            pltpu.VMEM((2, 3, levels, width), F32),
            pltpu.VMEM((2, 3, levels, width), F32),
            pltpu.VMEM((2, 2, levels, width), F32),
            pltpu.VMEM((2, 2, levels, width), F32),
            pltpu.VMEM((rows, width), F32),
            pltpu.VMEM((levs, rows, width), F32),
            pltpu.VMEM((4, width), F32),
            pltpu.VMEM((levs, 4, width), F32),
            pltpu.VMEM((2, 2, levels, width), F32),
            pltpu.VMEM((2, levels, width), F32),
            dma((6,)),
            dma((2,)),
            dma((2,)),
            dma((2,)),
            dma((2,)),
            dma((levs,)),
            dma((levs,)),
            dma((levs,)),
            dma((levs,)),
        ],
        compiler_params=pltpu.CompilerParams(
            collective_id=0, has_side_effects=True, vmem_limit_bytes=32 * 2**20
        ),
    )(*args)
    return pl.pallas_call(
        finish_kernel,
        name="finish",
        out_shape=[jax.ShapeDtypeStruct(slab, F32)] * 5,
        in_specs=[vmem] * 6,
        out_specs=[anywhere] * 5,
        scratch_shapes=[pltpu.VMEM(slab, F32)] * 3 + [dma((5,))],
        compiler_params=pltpu.CompilerParams(vmem_limit_bytes=16 * 2**20),
    )(*parts)


def solution(mesh):
    slab = P("lev", "lat", None)
    return jax.shard_map(
        body,
        mesh=mesh,
        in_specs=(slab,) * 4 + (P("lat", None), P()),
        out_specs=(slab,) * 5,
        check_vma=False,
    )
```

time: 70.6 us -> 22 us (0.31)
  starting transfers between devices: 24.4 us -> 0 us
  Pallas kernels: 0 us -> 21.2 us
  waiting for transfers between devices: 21 us -> 0 us
  local copies, waits for them, and re-layouts: 15.4 us -> 0 us
  other arithmetic: 7.65 us -> 0 us
    pallas_call x0 -> x2, Pallas kernels: none -> 21.2 us  [the longest x1 20 us: body(): pl.pallas_call(advect_kernel, name='advect', out_shape=[pltpu.VMEM(slab,...]
    all_to_all x2 -> x0, waiting for transfers between devices: 15.5 us -> none  [the longest x1 8.11 us: body(): lax.all_to_all(column_height, 'lev', split_axis=0, concat_axis=2, tiled=T...]
    ppermute x4 -> x0, starting transfers between devices: 14.1 us -> none  [the longest x2 10.3 us: with_halo(): before = lax.ppermute(last, axis, up)]
    all_to_all x2 -> x0, starting transfers between devices: 10.3 us -> none  [the longest x1 6.75 us: body(): lax.all_to_all(density_adjusted_heat, 'lev', split_axis=2, concat_axis=0,...]
    unnamed x20 -> x0, local copies, waits for them, and re-layouts: 5.72 us -> none
    ppermute x4 -> x0, waiting for transfers between devices: 5.44 us -> none  [the longest x2 5.43 us: with_halo(): after = lax.ppermute(initial, axis, down)]
    all_to_all x4 -> x0, local copies, waits for them, and re-layouts: 3.6 us -> none  [the longest x2 2.49 us: body(): lax.all_to_all(density_adjusted_heat, 'lev', split_axis=2, concat_axis=0,...]
    all_to_all x2 -> x0, other arithmetic: 2.72 us -> none  [the longest x1 1.36 us: body(): lax.all_to_all(column_height, 'lev', split_axis=0, concat_axis=2, tiled=T...]
  transfers between devices with their start and end apart: 6 -> 0, of which waited for: 4 -> 0; matrix products, arithmetic and copies ran while one was open for 5% -> 0% of each run, Pallas kernels for 0% -> 0%
where the time goes in v1:
time: 22 us; the launch traced here: 21.8 us
  Pallas kernels  21.2 us (96%)
  between operations  0.64 us (3%)
    pallas_call x1, Pallas kernels, body(): pl.pallas_call(advect_kernel, name='advect', out_shape=[pltpu.VMEM(slab,...  20 us
    pallas_call x1, Pallas kernels, body(): pl.pallas_call(finish_kernel, name='finish', out_shape=[jax.ShapeDtypeStr...  1.2 us

profile of v1, /device:TPU:225, one launch (start us, length us, event | category | flops | bytes accessed | tf_op | source)
XLA Modules:
  0.0 21.8 jit_solution(2192950755192437868)
XLA Ops:
  0.6 20.0 %advect.1 = (f32[8,16,576]{2,1,0:T(8,128)S(1)}, f32[8,16,576]{2,1,0:T(8,128)S(1)}, f32[8,16,576]{2,1,0:T(8,128)S(1)}, f32[8,16,576]{2,1,0:T(8,128)S(1)}, f32[8,1...) custom-call(f32[8,16,576]{2,1,0:T(8,128)} %u_hbm.1, f32[8,16,576]{2,1,0:T(8,128)} %v_hbm.1, f32[8,16,576]{2,1,0:T(8,128)} %t_hbm.1, ...), custom_call_target="tpu_custom_call" | custom-call | tf_op jit(solution)/shard_map/advect/pallas_call | solution.py:356
  20.6 1.2 %finish.1 = (f32[8,16,576]{2,1,0:T(8,128)}, f32[8,16,576]{2,1,0:T(8,128)}, f32[8,16,576]{2,1,0:T(8,128)}, f32[8,16,576]{2,1,0:T(8,128)}, f32[8,16,576]{2,1,0:T(8,128)}) custom-call(f32[8,16,576]{2,1,0:T(8,128)S(1)} %get-tuple-element.11.t_in, f32[8,16,576]{2,1,0:T(8,128)S(1)} %get-tuple-element.12.q_in, f32[8,16,576]{2,1,0:T(8,128)S(1)} %get-tuple-element.13.u_in, ...), custom_call_target="tpu_custom_call" | custom-call | tf_op jit(solution)/shard_map/finish/pallas_call | solution.py:390

commit v2 on v1

--- a/solution.py
+++ b/solution.py
@@ -57,38 +57,41 @@
     u_hbm, v_hbm, t_hbm, q_hbm, g_hbm, w_hbm,
     t_out, q_out, u_out, v_out, c_out, b_out,
     u_ref, v_ref, t_ref, q_ref, g_ref, w_ref,
-    raw_send, raw_recv, part_send, part_recv,
-    early_send, early_recv, late_send, late_recv, flux_ref, edge_ref,
-    in_sem, raw_ssem, raw_rsem, part_ssem, part_rsem,
-    early_ssem, early_rsem, late_ssem, late_rsem,
+    first_send, first_recv, rows_send, rows_recv, rest_send, rest_recv,
+    sum_send, meet_y, meet_x, total_send, pair_send, far_x, far_y,
+    late_send, late_recv, flux_ref, edge_ref,
+    in_sem, halo_ssem, halo_rsem, y_ssem, y_rsem, x_ssem, x_rsem, late_ssem, late_rsem,
 ):
     lat, lev = lax.axis_index("lat"), lax.axis_index("lev")
     lats, levs = lax.axis_size("lat"), lax.axis_size("lev")
+    along_y = meet_y.shape[0]
+    x, y = lev // along_y, lev % along_y
     levels, rows, width = t_ref.shape
+    half = rows // 2
     circle_sum = rows * lats
     full = width + (-width % 128)
     has_south, has_north = lat > 0, lat < lats - 1
 
     barrier = pltpu.get_barrier_semaphore()
 
+    def greet(band, slab):
+        pl.semaphore_signal(barrier, inc=1, device_id=(band, slab), device_id_type=MESH)
+
     @pl.when(has_south)
     def _():
-        pl.semaphore_signal(barrier, inc=1, device_id=(lat - 1, lev), device_id_type=MESH)
+        greet(lat - 1, lev)
 
     @pl.when(has_north)
     def _():
-        pl.semaphore_signal(barrier, inc=1, device_id=(lat + 1, lev), device_id_type=MESH)
-
-    def greet(step, carry):
-        pl.semaphore_signal(barrier, inc=1, device_id=(lat, lev + 1 + step), device_id_type=MESH)
-        return carry
-
-    lax.fori_loop(0, levs - 1 - lev, greet, 0)
+        greet(lat + 1, lev)
+
+    lax.fori_loop(0, levs - 1 - lev, lambda step, c: (greet(lat, lev + 1 + step), c)[1], 0)
+    lax.fori_loop(0, y, lambda step, c: (greet(lat, x * along_y + step), c)[1], 0)
 
     loads = [
         pltpu.make_async_copy(source, target, in_sem.at[n])
         for n, (source, target) in enumerate(
-            [(t_hbm, t_ref), (q_hbm, q_ref), (v_hbm, v_ref), (u_hbm, u_ref), (g_hbm, g_ref), (w_hbm, w_ref)]
+            [(v_hbm, v_ref), (t_hbm, t_ref), (q_hbm, q_ref), (u_hbm, u_ref), (g_hbm, g_ref), (w_hbm, w_ref)]
         )
     ]
     for load in loads:
@@ -107,72 +110,84 @@
     upper_wide = widen(upper, width)
     zonal_wide, merid_wide = widen(zonal, width), widen(merid, width)
 
-    def packed(ref, row):
-        return ref[:, row, :]
-
     def spread(row):
         return widen(jnp.broadcast_to(row, (levels, 128)), width)
 
-    if lats > 1:
-        @pl.when(jnp.logical_not(has_north))
-        def _():
-            raw_recv[0] = jnp.zeros(raw_recv.shape[1:], F32)
-            part_recv[0] = jnp.zeros(part_recv.shape[1:], F32)
-
-        @pl.when(jnp.logical_not(has_south))
-        def _():
-            raw_recv[1] = jnp.zeros(raw_recv.shape[1:], F32)
-            part_recv[1] = jnp.zeros(part_recv.shape[1:], F32)
-
-    for load in loads[:3]:
-        load.wait()
-
-    for side, row in ((0, 0), (1, rows - 1)):
-        raw_send[side, 0] = packed(v_ref, row)
-        raw_send[side, 1] = packed(t_ref, row)
-        raw_send[side, 2] = packed(q_ref, row)
-    pl.semaphore_wait(
-        barrier, lev + has_south.astype(jnp.int32) + has_north.astype(jnp.int32)
-    )
-
-    def halo(send, recv, ssem, rsem, side):
+    for side, exists in ((0, has_north), (1, has_south)):
+
+        @pl.when(jnp.logical_not(exists))
+        def _(side=side):
+            first_recv[side] = jnp.zeros(first_recv.shape[1:], F32)
+            rows_recv[side] = jnp.zeros(rows_recv.shape[1:], F32)
+            rest_recv[side] = jnp.zeros(rest_recv.shape[1:], F32)
+
+    def halo(kind, send, recv, side):
         return pltpu.make_async_remote_copy(
             src_ref=send.at[side],
             dst_ref=recv.at[side],
-            send_sem=ssem.at[side],
-            recv_sem=rsem.at[side],
+            send_sem=halo_ssem.at[kind, side],
+            recv_sem=halo_rsem.at[kind, side],
             device_id=(lat - 1 if side == 0 else lat + 1, lev),
             device_id_type=MESH,
         )
 
-    raw_copies = [halo(raw_send, raw_recv, raw_ssem, raw_rsem, side) for side in (0, 1)]
-    part_copies = [halo(part_send, part_recv, part_ssem, part_rsem, side) for side in (0, 1)]
-    pl.when(has_south)(raw_copies[0].start)
-    pl.when(has_north)(raw_copies[1].start)
+    halos = [
+        [halo(kind, send, recv, side) for side in (0, 1)]
+        for kind, (send, recv) in enumerate(
+            [(first_send, first_recv), (rows_send, rows_recv), (rest_send, rest_recv)]
+        )
+    ]
+
+    def start_halos(kind):
+        pl.when(has_south)(halos[kind][0].start)
+        pl.when(has_north)(halos[kind][1].start)
+
+    def wait_halos(kind):
+        pl.when(has_south)(halos[kind][1].wait_recv)
+        pl.when(has_north)(halos[kind][0].wait_recv)
+
+    for load in loads[:3]:
+        load.wait()
+
+    for side, row in ((0, 0), (1, rows - 1)):
+        first_send[side, 0] = v_ref[:, row, :]
+        first_send[side, 1] = t_ref[:, row, :] + MOIST_CORRECTION * q_ref[:, row, :]
+    pl.semaphore_wait(
+        barrier,
+        lev + along_y - 1 - y + has_south.astype(jnp.int32) + has_north.astype(jnp.int32),
+    )
+    start_halos(0)
 
     for load in loads[3:]:
         load.wait()
+    level_of = lax.broadcasted_iota(jnp.int32, (levels, 128), 0)
+    weights = jnp.zeros((levels, 128), F32)
+    for k in range(levels):
+        weights = jnp.where(level_of == k, w_ref[lev * levels + k], weights)
+    weights = widen(weights, width)
 
     for side, row, inner, interface, sign in (
         (0, 0, 1, upper[0:1], -1.0),
         (1, rows - 1, rows - 2, lower[rows - 1 :], 1.0),
     ):
-        tracer = raw_send[side, 1] + MOIST_CORRECTION * raw_send[side, 2]
-        tracer_in = packed(t_ref, inner) + MOIST_CORRECTION * packed(q_ref, inner)
-        wind_in = packed(v_ref, inner)
-        flux_in = spread(interface * 0.25) * (raw_send[side, 0] + wind_in) * (tracer + tracer_in)
-        wind = wrapped(packed(u_ref, row))
+        tracer = first_send[side, 1]
+        tracer_in = t_ref[:, inner, :] + MOIST_CORRECTION * q_ref[:, inner, :]
+        flux_in = (
+            spread(interface * 0.25) * (first_send[side, 0] + v_ref[:, inner, :]) * (tracer + tracer_in)
+        )
+        wind = wrapped(u_ref[:, row, :])
         around = wrapped(tracer)
         flux = 0.25 * (wind + east(wind)) * (around + east(around))
         change = (flux - west(flux, width))[:, :width]
-        part_send[side, 0] = (
+        part = (
             tracer
             - spread(zonal[row : row + 1]) * change
             + sign * spread(merid[row : row + 1]) * flux_in
         )
-        part_send[side, 1] = jnp.broadcast_to(g_ref[row : row + 1, :], (levels, width))
-    pl.when(has_south)(part_copies[0].start)
-    pl.when(has_north)(part_copies[1].start)
+        rest_send[side, 2] = part
+        rows_send[side, 0:1] = jnp.sum(weights * part, axis=0, keepdims=True)
+        rows_send[side, 1:2] = g_ref[row : row + 1, :]
+    start_halos(1)
 
     def partial(k, carry):
         zonal_sum, merid_sum, own_sum = carry
@@ -192,61 +207,110 @@
         levels,
         partial,
         (jnp.zeros((rows, full), F32), jnp.zeros((rows, width), F32), jnp.zeros((rows, width), F32)),
+        unroll=True,
     )
     north_sum = jnp.where(row_of < rows - 1, 0.25 * upper_wide * merid_sum, 0.0)
-    early_send[...] = (
+    slab_sum = (
         own_sum
         - zonal_wide * (0.25 * (zonal_sum - west(zonal_sum, width)))[:, :width]
         - merid_wide * (north_sum - pltpu.roll(north_sum, 1, 0))
     )
-
-    def exchange(send, recv, ssem, rsem, other):
+    sum_send[0] = slab_sum[:half]
+    sum_send[1] = slab_sum[half:]
+
+    def to_y(turn, step, source, target):
+        other = (y + step) % along_y
         return pltpu.make_async_remote_copy(
-            src_ref=send,
-            dst_ref=recv.at[lev],
-            send_sem=ssem.at[other],
-            recv_sem=rsem.at[lev],
+            src_ref=source,
+            dst_ref=target.at[y],
+            send_sem=y_ssem.at[turn, other],
+            recv_sem=y_rsem.at[turn, y],
+            device_id=(lat, x * along_y + other),
+            device_id_type=MESH,
+        )
+
+    def to_x(turn, other, source, target):
+        return pltpu.make_async_remote_copy(
+            src_ref=source,
+            dst_ref=target.at[x],
+            send_sem=x_ssem.at[turn, other],
+            recv_sem=x_rsem.at[turn, x],
+            device_id=(lat, other * along_y + y),
+            device_id_type=MESH,
+        )
+
+    def wait_slot(target, slot, sem):
+        pltpu.make_async_copy(target.at[slot], target.at[slot], sem).wait()
+
+    steps = sorted(range(1, along_y), key=lambda step: -min(step, along_y - step))
+    meets_y = [to_y(0, step, sum_send.at[0], meet_y) for step in steps]
+    for copy in meets_y:
+        copy.start()
+    lax.fori_loop(0, x, lambda other, c: (to_x(0, other, sum_send.at[1], meet_x).start(), c)[1], 0)
+
+    for side, row in ((0, 0), (1, rows - 1)):
+        rest_send[side, 0] = t_ref[:, row, :]
+        rest_send[side, 1] = q_ref[:, row, :]
+    start_halos(2)
+
+    wait_halos(0)
+    wait_halos(1)
+    for side, interface in ((0, north_interface), (1, south_interface)):
+        mine = 1 - side
+        wind = spread(interface * 0.25) * (first_send[mine, 0] + first_recv[side, 0])
+        flux = wind * (first_send[mine, 1] + first_recv[side, 1])
+        late_send[side : side + 1] = jnp.sum(weights * flux, axis=0, keepdims=True)
+        late_send[side + 2 : side + 3] = rows_recv[side, 0:1]
+
+    def to_lower(other):
+        return pltpu.make_async_remote_copy(
+            src_ref=late_send,
+            dst_ref=late_recv.at[lev],
+            send_sem=late_ssem.at[other],
+            recv_sem=late_rsem.at[lev],
             device_id=(lat, other),
             device_id_type=MESH,
         )
 
-    def send_early(other, carry):
-        exchange(early_send, early_recv, early_ssem, early_rsem, other).start()
-        return carry
-
-    lax.fori_loop(0, lev, send_early, 0)
-
-    pl.when(has_south)(raw_copies[1].wait_recv)
-    pl.when(has_north)(raw_copies[0].wait_recv)
-    for side, interface in ((0, north_interface), (1, south_interface)):
+    lax.fori_loop(0, lev, lambda other, c: (to_lower(other).start(), c)[1], 0)
+
+    below_y = jnp.zeros((half, width), F32)
+    total_y = sum_send[0]
+    for step in range(1, along_y):
+        other = (y + step) % along_y
+        wait_slot(meet_y, other, y_rsem.at[0, other])
+        came = meet_y[other]
+        total_y += came
+        below_y += jnp.where(y + step < along_y, came, 0.0)
+    total_send[...] = total_y
+    lax.fori_loop(0, x, lambda other, c: (to_x(1, other, total_send, far_x).start(), c)[1], 0)
+
+    def add_x(turn, target):
+        def add(other, total):
+            wait_slot(target, other, x_rsem.at[turn, other])
+            return total + target[other]
+
+        return add
+
+    below_x = lax.fori_loop(x + 1, levs // along_y, add_x(0, meet_x), jnp.zeros((half, width), F32))
+    pair_send[0] = below_x
+    pair_send[1] = below_x + sum_send[1]
+    fars_y = [to_y(1, step, pair_send.at[(y + step) // along_y], far_y) for step in steps]
+    for copy in fars_y:
+        copy.start()
+
+    wait_halos(2)
+    for side, exists, interface, merid_edge, sign in (
+        (0, has_north, north_interface, merid_north, 1.0),
+        (1, has_south, south_interface, merid_south, -1.0),
+    ):
         mine = 1 - side
-        wind = spread(interface * 0.25) * (raw_send[mine, 0] + raw_recv[side, 0])
-        flux_ref[side, 0] = wind * (raw_send[mine, 1] + raw_recv[side, 1])
-        flux_ref[side, 1] = wind * (raw_send[mine, 2] + raw_recv[side, 2])
-    level_of = lax.broadcasted_iota(jnp.int32, (levels, 128), 0)
-    weights = jnp.zeros((levels, 128), F32)
-    for k in range(levels):
-        weights = jnp.where(level_of == k, w_ref[lev * levels + k], weights)
-    weights = widen(weights, width)
-    pl.when(has_south)(part_copies[1].wait_recv)
-    pl.when(has_north)(part_copies[0].wait_recv)
-    for side, exists, merid_edge, sign in (
-        (0, has_north, merid_north, 1.0),
-        (1, has_south, merid_south, -1.0),
-    ):
+        wind = spread(interface * 0.25) * (first_send[mine, 0] + first_recv[side, 0])
+        flux_ref[side, 0] = wind * (rest_send[mine, 0] + rest_recv[side, 0])
+        flux_ref[side, 1] = wind * (rest_send[mine, 1] + rest_recv[side, 1])
         flux = flux_ref[side, 0] + MOIST_CORRECTION * flux_ref[side, 1]
-        part = part_recv[side, 0]
-        late_send[side : side + 1] = jnp.sum(weights * flux, axis=0, keepdims=True)
-        late_send[side + 2 : side + 3] = jnp.sum(weights * part, axis=0, keepdims=True)
-        beyond = weights * (part + sign * spread(merid_edge) * flux)
+        beyond = weights * (rest_recv[side, 2] + sign * spread(merid_edge) * flux)
         edge_ref[side] = jnp.where(exists, beyond, 0.0)
-
-    def send_late(other, carry):
-        exchange(late_send, late_recv, late_ssem, late_rsem, other).start()
-        return carry
-
-    lax.fori_loop(0, lev, send_late, 0)
-
     half_zonal = 0.5 * zonal_wide
 
     def local(step, carry):
@@ -286,24 +350,28 @@
         levels,
         local,
         (jnp.zeros((rows, width), F32), jnp.zeros((1, width), F32), jnp.zeros((1, width), F32)),
-    )
-
-    def add_early(other, total):
-        pltpu.make_async_copy(early_recv.at[other], early_recv.at[other], early_rsem.at[other]).wait()
-        return total + early_recv[other]
+        unroll=2,
+    )
+
+    south_half = lax.fori_loop(x + 1, levs // along_y, add_x(1, far_x), below_y)
+    north_half = below_x
+    for step in range(1, along_y):
+        other = (y + step) % along_y
+        wait_slot(far_y, other, y_rsem.at[1, other])
+        north_half += far_y[other]
+    total = g_ref[...] + jnp.concatenate([south_half, north_half], axis=0)
 
     def add_late(other, total):
-        pltpu.make_async_copy(late_recv.at[other], late_recv.at[other], late_rsem.at[other]).wait()
+        wait_slot(late_recv, other, late_rsem.at[other])
         return total + late_recv[other]
 
-    total = lax.fori_loop(lev + 1, levs, add_early, g_ref[...])
     edges = lax.fori_loop(lev + 1, levs, add_late, jnp.zeros(late_send.shape, F32))
     north_flux, south_flux = edges[0:1], edges[1:2]
     total = total + merid_wide * (
         jnp.where(row_of == 0, south_flux, 0.0) - jnp.where(row_of == rows - 1, north_flux, 0.0)
     )
-    beyond_north = part_recv[0, 1, 0:1] + edges[2:3] + widen(merid_north, width) * north_flux
-    beyond_south = part_recv[1, 1, 0:1] + edges[3:4] - widen(merid_south, width) * south_flux
+    beyond_north = rows_recv[0, 1:2] + edges[2:3] + widen(merid_north, width) * north_flux
+    beyond_south = rows_recv[1, 1:2] + edges[3:4] - widen(merid_south, width) * south_flux
     beyond_north = jnp.where(has_north, beyond_north, 0.0)
     beyond_south = jnp.where(has_south, beyond_south, 0.0)
     around = wrapped(total)
@@ -313,16 +381,14 @@
     south = jnp.where(row_of == 0, beyond_south, pltpu.roll(total, 1, 0))
     b_out[2] = 0.5 * MERID_RATE * (north - south)
 
-    for side, exists in ((0, has_south), (1, has_north)):
-        pl.when(exists)(raw_copies[side].wait_send)
-        pl.when(exists)(part_copies[side].wait_send)
-
-    def sent(other, carry):
-        exchange(early_send, early_recv, early_ssem, early_rsem, other).wait_send()
-        exchange(late_send, late_recv, late_ssem, late_rsem, other).wait_send()
-        return carry
-
-    lax.fori_loop(0, lev, sent, 0)
+    for kind in range(3):
+        pl.when(has_south)(halos[kind][0].wait_send)
+        pl.when(has_north)(halos[kind][1].wait_send)
+    for copy in meets_y + fars_y:
+        copy.wait_send()
+    lax.fori_loop(0, x, lambda other, c: (to_x(0, other, sum_send.at[1], meet_x).wait_send(), c)[1], 0)
+    lax.fori_loop(0, x, lambda other, c: (to_x(1, other, total_send, far_x).wait_send(), c)[1], 0)
+    lax.fori_loop(0, lev, lambda other, c: (to_lower(other).wait_send(), c)[1], 0)
 
 
 def finish_kernel(t_in, q_in, u_in, v_in, c_in, b_in, t, q, u, v, h, u_new, v_new, h_new, sems):
@@ -348,6 +414,8 @@
 def body(zonal, poleward, heat, humidity, ground, weights):
     levels, rows, width = heat.shape
     levs = lax.axis_size("lev")
+    along_y = 4 if levs % 4 == 0 else levs
+    along_x, half = levs // along_y, rows // 2
     slab = (levels, rows, width)
     anywhere = pl.BlockSpec(memory_space=pl.ANY)
     vmem = pl.BlockSpec(memory_space=pltpu.VMEM)
@@ -363,23 +431,30 @@
         + [
             pltpu.VMEM((rows, width), F32),
             pltpu.SMEM(weights.shape, F32),
+            pltpu.VMEM((2, 2, levels, width), F32),
+            pltpu.VMEM((2, 2, levels, width), F32),
+            pltpu.VMEM((2, 2, width), F32),
+            pltpu.VMEM((2, 2, width), F32),
             pltpu.VMEM((2, 3, levels, width), F32),
             pltpu.VMEM((2, 3, levels, width), F32),
-            pltpu.VMEM((2, 2, levels, width), F32),
-            pltpu.VMEM((2, 2, levels, width), F32),
-            pltpu.VMEM((rows, width), F32),
-            pltpu.VMEM((levs, rows, width), F32),
+            pltpu.VMEM((2, half, width), F32),
+            pltpu.VMEM((along_y, half, width), F32),
+            pltpu.VMEM((along_x, half, width), F32),
+            pltpu.VMEM((half, width), F32),
+            pltpu.VMEM((2, half, width), F32),
+            pltpu.VMEM((along_x, half, width), F32),
+            pltpu.VMEM((along_y, half, width), F32),
             pltpu.VMEM((4, width), F32),
             pltpu.VMEM((levs, 4, width), F32),
             pltpu.VMEM((2, 2, levels, width), F32),
             pltpu.VMEM((2, levels, width), F32),
             dma((6,)),
-            dma((2,)),
-            dma((2,)),
-            dma((2,)),
-            dma((2,)),
-            dma((levs,)),
-            dma((levs,)),
+            dma((3, 2)),
+            dma((3, 2)),
+            dma((2, along_y)),
+            dma((2, along_y)),
+            dma((2, along_x)),
+            dma((2, along_x)),
             dma((levs,)),
             dma((levs,)),
         ],

time: 22 us -> 19.2 us (0.87)
  the two profiles are of different devices: /device:TPU:225 before, /device:TPU:2 now
where the time goes in v2:
time: 19.2 us; the launch traced here: 19.1 us
  Pallas kernels  18.4 us (96%)
  between operations  0.64 us (3%)
    pallas_call x1, Pallas kernels, body(): pl.pallas_call(advect_kernel, name='advect', out_shape=[pltpu.VMEM(slab,...  17.2 us
    pallas_call x1, Pallas kernels, body(): pl.pallas_call(finish_kernel, name='finish', out_shape=[jax.ShapeDtypeStr...  1.2 us

profile of v2, /device:TPU:2, one launch (start us, length us, event | category | flops | bytes accessed | tf_op | source)
XLA Modules:
  0.0 19.1 jit_solution(398429420309177087)
XLA Ops:
  0.6 17.2 %advect.1 = (f32[8,16,576]{2,1,0:T(8,128)S(1)}, f32[8,16,576]{2,1,0:T(8,128)S(1)}, f32[8,16,576]{2,1,0:T(8,128)S(1)}, f32[8,16,576]{2,1,0:T(8,128)S(1)}, f32[8,1...) custom-call(f32[8,16,576]{2,1,0:T(8,128)} %u_hbm.1, f32[8,16,576]{2,1,0:T(8,128)} %v_hbm.1, f32[8,16,576]{2,1,0:T(8,128)} %t_hbm.1, ...), custom_call_target="tpu_custom_call" | custom-call | tf_op jit(solution)/shard_map/advect/pallas_call | solution.py:424
  17.9 1.2 %finish.1 = (f32[8,16,576]{2,1,0:T(8,128)}, f32[8,16,576]{2,1,0:T(8,128)}, f32[8,16,576]{2,1,0:T(8,128)}, f32[8,16,576]{2,1,0:T(8,128)}, f32[8,16,576]{2,1,0:T(8,128)}) custom-call(f32[8,16,576]{2,1,0:T(8,128)S(1)} %get-tuple-element.11.t_in, f32[8,16,576]{2,1,0:T(8,128)S(1)} %get-tuple-element.12.q_in, f32[8,16,576]{2,1,0:T(8,128)S(1)} %get-tuple-element.13.u_in, ...), custom_call_target="tpu_custom_call" | custom-call | tf_op jit(solution)/shard_map/finish/pallas_call | solution.py:465

commit v3 on v2

v3 whole, which is shorter than its diff:
```python
import functools
import jax
import jax.numpy as jnp
from jax import lax
from jax.experimental import pallas as pl
from jax.experimental.pallas import tpu as pltpu
from jax.sharding import PartitionSpec as P

ZONAL_RATE = 0.1
MERID_RATE = 0.25
POLAR_CAP = 0.2
MOIST_CORRECTION = 0.6
F32 = jnp.float32
MESH = pl.DeviceIdType.MESH


def lat_weights(row_index, circle_sum):
    spacing = jnp.pi / circle_sum
    middle_boxes = jnp.cos(-jnp.pi / 2 + (row_index + 0.5) * spacing)
    upper_interface = jnp.where(
        row_index + 1.0 < circle_sum, jnp.cos(-jnp.pi / 2 + (row_index + 1.0) * spacing), 0.0
    )
    lower_interface = jnp.where(row_index > 0.5, jnp.cos(-jnp.pi / 2 + row_index * spacing), 0.0)
    return middle_boxes, upper_interface, lower_interface


def widen(column, width):
    whole, rest = width // 128, width % 128
    parts = [column] * whole + ([column[:, :rest]] if rest else [])
    return jnp.concatenate(parts, axis=1)


def wrapped(value):
    width = value.shape[1]
    extra = -width % 128
    if extra == 0:
        return value
    return jnp.concatenate([value, value[:, :extra]], axis=1)


def east(full):
    return pltpu.roll(full, full.shape[1] - 1, 1)


def west(full, width):
    size = full.shape[1]
    rolled = pltpu.roll(full, 1, 1)
    if size == width:
        return rolled
    last = pltpu.roll(full[:, size - 128 :], 128 - (width - 1 - (size - 128)), 1)
    lane = lax.broadcasted_iota(jnp.int32, last.shape, 1)
    start = jnp.where(lane == 0, last, rolled[:, :128])
    return jnp.concatenate([start, rolled[:, 128:]], axis=1)


def advect_kernel(
    u_hbm, v_hbm, t_hbm, q_hbm, g_hbm, w_hbm,
    t_out, q_out, u_out, v_out, c_out, b_out,
    u_ref, v_ref, t_ref, q_ref, g_ref, w_ref, edge_rows,
    first_send, first_recv, rows_send, rows_recv, rest_send, rest_recv,
    sum_send, meet_y, total_send, far_x, meet_x, pair_send, far_y, hold_ref,
    late_send, late_recv,
    in_sem, edge_sem, halo_ssem, halo_rsem, y_ssem, y_rsem, x_ssem, x_rsem, late_ssem, late_rsem, ready,
):
    lat, lev = lax.axis_index("lat"), lax.axis_index("lev")
    lats, levs = lax.axis_size("lat"), lax.axis_size("lev")
    along_y = meet_y.shape[1]
    x, y = lev // along_y, lev % along_y
    levels, rows, width = t_ref.shape
    half = rows // 2
    circle_sum = rows * lats
    full = width + (-width % 128)
    has_south, has_north = lat > 0, lat < lats - 1

    barrier = pltpu.get_barrier_semaphore()
    first_band = lat == 0
    first = first_band & (lev == 0)

    def greet(band, slab):
        pl.semaphore_signal(barrier, inc=1, device_id=(band, slab), device_id_type=MESH)

    @pl.when(has_south)
    def _():
        greet(lat - 1, lev)

    @pl.when(has_north)
    def _():
        greet(lat + 1, lev)

    pl.when(first_band & (lev > 0))(lambda: greet(lat, 0))

    @pl.when(jnp.logical_not(first))
    def _():
        lax.fori_loop(lev + 1, levs, lambda slab, c: (greet(lat, slab), c)[1], 0)
        known = jnp.maximum(x * along_y, first_band.astype(jnp.int32))
        lax.fori_loop(known, lev, lambda slab, c: (greet(lat, slab), c)[1], 0)

    edge_loads = [
        pltpu.make_async_copy(
            source.at[:, pl.ds(side * (rows - 2), 2), :], edge_rows.at[kind, side], edge_sem.at[kind, side]
        )
        for kind, source in enumerate([v_hbm, t_hbm, q_hbm, u_hbm])
        for side in (0, 1)
    ]
    loads = [
        pltpu.make_async_copy(source, target, in_sem.at[n])
        for n, (source, target) in enumerate(
            [(w_hbm, w_ref), (g_hbm, g_ref), (t_hbm, t_ref), (q_hbm, q_ref), (u_hbm, u_ref), (v_hbm, v_ref)]
        )
    ]
    for load in edge_loads + loads[:2]:
        load.start()

    band = (lat * rows + lax.broadcasted_iota(jnp.int32, (rows, 128), 0)).astype(F32)
    centre, upper, lower = lat_weights(band, circle_sum)
    zonal = ZONAL_RATE / jnp.maximum(centre, POLAR_CAP)
    merid = MERID_RATE / centre
    beside = lat * rows - 1 + (rows + 1) * lax.broadcasted_iota(jnp.int32, (8, 128), 0)
    beside_centre, _, _ = lat_weights(beside.astype(F32), circle_sum)
    merid_beside = MERID_RATE / beside_centre
    south_interface, north_interface = lower[0:1], upper[rows - 1 :]
    merid_south, merid_north = merid_beside[0:1], merid_beside[1:2]
    row_of = lax.broadcasted_iota(jnp.int32, (rows, width), 0)
    upper_wide = widen(upper, width)
    zonal_wide, merid_wide = widen(zonal, width), widen(merid, width)

    def spread(row):
        return widen(jnp.broadcast_to(row, (levels, 128)), width)

    for side, exists in ((0, has_north), (1, has_south)):

        @pl.when(jnp.logical_not(exists))
        def _(side=side):
            first_recv[side] = jnp.zeros(first_recv.shape[1:], F32)
            rows_recv[side] = jnp.zeros(rows_recv.shape[1:], F32)
            rest_recv[side] = jnp.zeros(rest_recv.shape[1:], F32)

    def halo(kind, send, recv, side):
        return pltpu.make_async_remote_copy(
            src_ref=send.at[side],
            dst_ref=recv.at[side],
            send_sem=halo_ssem.at[kind, side],
            recv_sem=halo_rsem.at[kind, side],
            device_id=(lat - 1 if side == 0 else lat + 1, lev),
            device_id_type=MESH,
        )

    halos = [
        [halo(kind, send, recv, side) for side in (0, 1)]
        for kind, (send, recv) in enumerate(
            [(first_send, first_recv), (rows_send, rows_recv), (rest_send, rest_recv)]
        )
    ]

    def start_halos(kind):
        pl.when(has_south)(halos[kind][0].start)
        pl.when(has_north)(halos[kind][1].start)

    def wait_halos(kind):
        pl.when(has_south)(halos[kind][1].wait_recv)
        pl.when(has_north)(halos[kind][0].wait_recv)

    for load in edge_loads:
        load.wait()
    for load in loads[2:]:
        load.start()

    def edge_row(kind, side, inner=False):
        return edge_rows[kind, side, :, side if not inner else 1 - side, :]

    for side in (0, 1):
        first_send[side, 0] = edge_row(0, side)
        first_send[side, 1] = edge_row(1, side) + MOIST_CORRECTION * edge_row(2, side)
    pl.semaphore_wait(
        barrier,
        jnp.where(first, levs - 1, lev - first_band.astype(jnp.int32) + along_y - 1 - y)
        + has_south.astype(jnp.int32)
        + has_north.astype(jnp.int32),
    )
    start_halos(0)

    @pl.when(first)
    def _():
        def answer(slab, carry):
            pl.semaphore_signal(ready, inc=1, device_id=(lat, slab), device_id_type=MESH)
            return carry

        lax.fori_loop(1, levs, answer, 0)

    for load in loads[:2]:
        load.wait()
    level_of = lax.broadcasted_iota(jnp.int32, (levels, 128), 0)
    weights = jnp.zeros((levels, 128), F32)
    for k in range(levels):
        weights = jnp.where(level_of == k, w_ref[lev * levels + k], weights)
    weights = widen(weights, width)

    for side, row, interface, sign in (
        (0, 0, upper[0:1], -1.0),
        (1, rows - 1, lower[rows - 1 :], 1.0),
    ):
        tracer = first_send[side, 1]
        tracer_in = edge_row(1, side, True) + MOIST_CORRECTION * edge_row(2, side, True)
        flux_in = (
            spread(interface * 0.25)
            * (first_send[side, 0] + edge_row(0, side, True))
            * (tracer + tracer_in)
        )
        wind = wrapped(edge_row(3, side))
        around = wrapped(tracer)
        flux = 0.25 * (wind + east(wind)) * (around + east(around))
        change = (flux - west(flux, width))[:, :width]
        part = (
            tracer
            - spread(zonal[row : row + 1]) * change
            + sign * spread(merid[row : row + 1]) * flux_in
        )
        rest_send[side, 0] = edge_row(1, side)
        rest_send[side, 1] = edge_row(2, side)
        rest_send[side, 2] = part
        rows_send[side, 0:1] = jnp.sum(weights * part, axis=0, keepdims=True)
        rows_send[side, 1:2] = g_ref[row : row + 1, :]
    start_halos(1)
    start_halos(2)
    for load in loads[2:]:
        load.wait()

    def partial(k, carry):
        zonal_sum, merid_sum, own_sum = carry
        weight = w_ref[lev * levels + k]
        tracer = t_ref[k] + MOIST_CORRECTION * q_ref[k]
        around = wrapped(tracer)
        wind = wrapped(u_ref[k])
        zonal_sum += weight * ((wind + east(wind)) * (around + east(around)))
        cross = v_ref[k]
        merid_sum += weight * (
            (cross + pltpu.roll(cross, rows - 1, 0)) * (tracer + pltpu.roll(tracer, rows - 1, 0))
        )
        return zonal_sum, merid_sum, own_sum + weight * tracer

    zonal_sum, merid_sum, own_sum = lax.fori_loop(
        0,
        levels,
        partial,
        (jnp.zeros((rows, full), F32), jnp.zeros((rows, width), F32), jnp.zeros((rows, width), F32)),
        unroll=True,
    )
    north_sum = jnp.where(row_of < rows - 1, 0.25 * upper_wide * merid_sum, 0.0)
    slab_sum = (
        own_sum
        - zonal_wide * (0.25 * (zonal_sum - west(zonal_sum, width)))[:, :width]
        - merid_wide * (north_sum - pltpu.roll(north_sum, 1, 0))
    )

    sum_send[0] = slab_sum[:half]
    sum_send[1] = slab_sum[half:]

    def along(ssem, rsem, source, target, here, leg, other, slab):
        return pltpu.make_async_remote_copy(
            src_ref=source,
            dst_ref=target.at[here],
            send_sem=ssem.at[leg, other],
            recv_sem=rsem.at[leg, here],
            device_id=(lat, slab),
            device_id_type=MESH,
        )

    def to_y(leg, source, target, other):
        return along(y_ssem, y_rsem, source, target, y, leg, other, x * along_y + other)

    def to_x(leg, source, target, other):
        return along(x_ssem, x_rsem, source, target, x, leg, other, other * along_y + y)

    def wait_slot(target, slot, sem):
        pltpu.make_async_copy(target.at[slot], target.at[slot], sem).wait()

    def start(copy):
        copy.start()

    def wait_send(copy):
        copy.wait_send()

    steps = sorted(range(1, along_y), key=lambda step: -min(step, along_y - step))
    swapped = jnp.logical_not(first_band)

    def meet_along_y(part, act):
        for step in steps:
            other = (y + step) % along_y
            wanted = (x > 0) | ((other < y) & ((other > 0) | swapped))
            pl.when(wanted)(lambda other=other: act(to_y(part, sum_send.at[part], meet_y.at[part], other)))

    def meet_along_x(act):
        lax.fori_loop(0, x, lambda other, c: (act(to_x(2, sum_send.at[1], meet_x, other)), c)[1], 0)

    def far_along_x(part, act):
        begin = jnp.where(first_band & (y == 0), 1, 0)
        lax.fori_loop(
            begin, x, lambda other, c: (act(to_x(part, total_send.at[part], far_x.at[part], other)), c)[1], 0
        )

    def far_along_y(act):
        for step in steps:
            other = (y + step) % along_y
            act(to_y(2, pair_send.at[(y + step) // along_y], far_y, other))

    def to_first(act):
        @pl.when(first_band & (x == 0) & (y > 0))
        def _():
            for part in (0, 1):
                act(to_y(part, sum_send.at[part], meet_y.at[part], 0))

        @pl.when(first_band & (x > 0) & (y == 0))
        def _():
            for part in (0, 1):
                act(to_x(part, total_send.at[part], far_x.at[part], 0))

        pl.when(first_band & (lev > 0))(lambda: act(to_lower(0)))

    def to_lower(other):
        return pltpu.make_async_remote_copy(
            src_ref=late_send,
            dst_ref=late_recv.at[lev],
            send_sem=late_ssem.at[other],
            recv_sem=late_rsem.at[lev],
            device_id=(lat, other),
            device_id_type=MESH,
        )

    def late_to_lower(act):
        lax.fori_loop(
            first_band.astype(jnp.int32), lev, lambda other, c: (act(to_lower(other)), c)[1], 0
        )

    meet_along_y(0, start)
    pl.when(first_band)(lambda: meet_along_y(1, start))
    pl.when(swapped)(lambda: meet_along_x(start))

    @pl.when(lev > 0)
    def _():
        wait_halos(0)
        wait_halos(1)
        for side, interface in ((0, north_interface), (1, south_interface)):
            mine = 1 - side
            wind = spread(interface * 0.25) * (first_send[mine, 0] + first_recv[side, 0])
            flux = wind * (first_send[mine, 1] + first_recv[side, 1])
            late_send[side : side + 1] = jnp.sum(weights * flux, axis=0, keepdims=True)
            late_send[side + 2 : side + 3] = rows_recv[side, 0:1]
        late_to_lower(start)

    def second_along_x(part):
        below, total_y = jnp.zeros((half, width), F32), sum_send[part]
        for step in range(1, along_y):
            other = (y + step) % along_y
            comes = (x > 0) | (other > y)

            @pl.when(comes)
            def _(other=other):
                wait_slot(meet_y.at[part], other, y_rsem.at[part, other])

            came = jnp.where(comes, meet_y[part, other], 0.0)
            total_y += came
            below += jnp.where(other > y, came, 0.0)
        total_send[part] = total_y
        hold_ref[part] = below
        far_along_x(part, start)

    def second_along_y():
        def add(other, total):
            wait_slot(meet_x, other, x_rsem.at[2, other])
            return total + meet_x[other]

        below = lax.fori_loop(x + 1, levs // along_y, add, jnp.zeros((half, width), F32))
        hold_ref[1] = below
        pair_send[0] = below
        pair_send[1] = below + sum_send[1]
        far_along_y(start)

    second_along_x(0)
    pl.when(first_band)(lambda: second_along_x(1))
    pl.when(swapped)(second_along_y)

    @pl.when(first_band & (lev > 0))
    def _():
        pl.semaphore_wait(ready, 1)

    to_first(start)

    half_zonal = 0.5 * zonal_wide
    inner_upper = jnp.where(row_of < rows - 1, 0.25 * upper_wide, 0.0)

    def local(step, below):
        k = levels - 1 - step
        weight = w_ref[lev * levels + k]
        wind, cross = u_ref[k], v_ref[k]
        wind_full = wrapped(wind)
        wind_pair = 0.25 * (wind_full + east(wind_full))
        cross_pair = inner_upper * (cross + pltpu.roll(cross, rows - 1, 0))

        def moved(tracer):
            around = wrapped(tracer)
            flux = wind_pair * (around + east(around))
            change = (flux - west(flux, width))[:, :width]
            north = cross_pair * (tracer + pltpu.roll(tracer, rows - 1, 0))
            return tracer - zonal_wide * change - merid_wide * (north - pltpu.roll(north, 1, 0))

        heat, humid = moved(t_ref[k]), moved(q_ref[k])
        t_out[k] = heat
        q_out[k] = humid
        below = below + weight * (heat + MOIST_CORRECTION * humid)
        c_out[k] = below
        around = wrapped(below)
        u_out[k] = wind - half_zonal * (east(around) - west(around, width))[:, :width]
        north = jnp.where(row_of == rows - 1, 0.0, pltpu.roll(below, rows - 1, 0))
        south = jnp.where(row_of == 0, 0.0, pltpu.roll(below, 1, 0))
        v_out[k] = cross - 0.5 * MERID_RATE * (north - south)
        return below

    lax.fori_loop(0, levels, local, jnp.zeros((rows, width), F32), unroll=2)

    def from_below(value):
        reach = 1
        while reach < levels:
            lower_part = pltpu.roll(value, levels - reach, 0)
            value = value + jnp.where(level_wide + reach < levels, lower_part, 0.0)
            reach *= 2
        return value

    level_wide = lax.broadcasted_iota(jnp.int32, (levels, width), 0)
    pl.when(lev == 0)(lambda: (wait_halos(0), wait_halos(1), None)[-1])
    wait_halos(2)
    for side, exists, row, beside_row, interface, merid_edge, sign in (
        (0, has_north, rows - 1, rows - 2, north_interface, merid_north, 1.0),
        (1, has_south, 0, 1, south_interface, merid_south, -1.0),
    ):
        mine = 1 - side
        wind = spread(interface * 0.25) * (first_send[mine, 0] + first_recv[side, 0])
        heat_flux = wind * (rest_send[mine, 0] + rest_recv[side, 0])
        humid_flux = wind * (rest_send[mine, 1] + rest_recv[side, 1])
        out = sign * spread(merid[row : row + 1])
        t_out[:, row, :] = t_out[:, row, :] - out * heat_flux
        q_out[:, row, :] = q_out[:, row, :] - out * humid_flux
        flux = heat_flux + MOIST_CORRECTION * humid_flux
        edge = from_below(weights * out * flux)
        beyond = weights * (rest_recv[side, 2] + sign * spread(merid_edge) * flux)
        beyond = from_below(jnp.where(exists, beyond, 0.0))
        c_out[:, row, :] = c_out[:, row, :] - edge
        around = wrapped(edge)
        turn = (east(around) - west(around, width))[:, :width]
        u_out[:, row, :] = u_out[:, row, :] + 0.5 * spread(zonal[row : row + 1]) * turn
        across = 0.5 * MERID_RATE * sign
        v_out[:, row, :] = v_out[:, row, :] - across * beyond
        v_out[:, beside_row, :] = v_out[:, beside_row, :] + across * edge

    def last_along_x(part):
        def add(other, total):
            wait_slot(far_x.at[part], other, x_rsem.at[part, other])
            return total + far_x[part, other]

        hold_ref[part] = lax.fori_loop(x + 1, levs // along_y, add, hold_ref[part])

    def last_along_y():
        total = hold_ref[1]
        for step in range(1, along_y):
            other = (y + step) % along_y
            wait_slot(far_y, other, y_rsem.at[2, other])
            total += far_y[other]
        hold_ref[1] = total

    last_along_x(0)
    pl.when(first_band)(lambda: last_along_x(1))
    pl.when(swapped)(last_along_y)
    total = g_ref[...] + jnp.concatenate([hold_ref[0], hold_ref[1]], axis=0)

    around = wrapped(total)
    b_out[0] = total
    b_out[1] = half_zonal * (east(around) - west(around, width))[:, :width]
    north = jnp.where(row_of == rows - 1, 0.0, pltpu.roll(total, rows - 1, 0))
    south = jnp.where(row_of == 0, 0.0, pltpu.roll(total, 1, 0))
    b_out[2] = 0.5 * MERID_RATE * (north - south)

    def add_late(other, total):
        wait_slot(late_recv, other, late_rsem.at[other])
        return total + late_recv[other]

    edges = lax.fori_loop(lev + 1, levs, add_late, jnp.zeros(late_send.shape, F32))
    for side, exists, row, beside_row, merid_edge, sign in (
        (0, has_north, rows - 1, rows - 2, merid_north, 1.0),
        (1, has_south, 0, 1, merid_south, -1.0),
    ):
        flux = edges[side : side + 1]
        change = -sign * merid_wide[row : row + 1] * flux
        beyond = rows_recv[side, 1:2] + edges[side + 2 : side + 3] + sign * widen(merid_edge, width) * flux
        around = wrapped(change)
        turn = (east(around) - west(around, width))[:, :width]
        across = 0.5 * MERID_RATE * sign
        b_out[0, row : row + 1] += change
        b_out[1, row : row + 1] += half_zonal[row : row + 1] * turn
        b_out[2, row : row + 1] += across * jnp.where(exists, beyond, 0.0)
        b_out[2, beside_row : beside_row + 1] += across * change

    for kind in range(3):
        pl.when(has_south)(halos[kind][0].wait_send)
        pl.when(has_north)(halos[kind][1].wait_send)
    meet_along_y(0, wait_send)
    far_along_x(0, wait_send)

    @pl.when(first_band)
    def _():
        meet_along_y(1, wait_send)
        far_along_x(1, wait_send)

    @pl.when(swapped)
    def _():
        meet_along_x(wait_send)
        far_along_y(wait_send)

    to_first(wait_send)
    late_to_lower(wait_send)


def finish_kernel(t_in, q_in, u_in, v_in, c_in, b_in, t, q, u, v, h, u_new, v_new, h_new, sems):
    copies = [
        pltpu.make_async_copy(source, target, sems.at[n])
        for n, (source, target) in enumerate([(t_in, t), (q_in, q), (h_new, h), (u_new, u), (v_new, v)])
    ]
    copies[0].start()
    copies[1].start()
    for k in range(t_in.shape[0]):
        h_new[k] = c_in[k] + b_in[0]
    copies[2].start()
    for k in range(t_in.shape[0]):
        u_new[k] = u_in[k] - b_in[1]
    copies[3].start()
    for k in range(t_in.shape[0]):
        v_new[k] = v_in[k] - b_in[2]
    copies[4].start()
    for copy in copies:
        copy.wait()


def body(zonal, poleward, heat, humidity, ground, weights):
    levels, rows, width = heat.shape
    levs = lax.axis_size("lev")
    along_y = 4 if levs % 4 == 0 else levs
    along_x, half = levs // along_y, rows // 2
    slab = (levels, rows, width)
    anywhere = pl.BlockSpec(memory_space=pl.ANY)
    vmem = pl.BlockSpec(memory_space=pltpu.VMEM)
    dma = pltpu.SemaphoreType.DMA
    args = [pltpu.with_memory_space_constraint(x, pltpu.HBM) for x in (zonal, poleward, heat, humidity, ground, weights)]
    parts = pl.pallas_call(
        advect_kernel,
        name="advect",
        out_shape=[pltpu.VMEM(slab, F32)] * 5 + [pltpu.VMEM((3, rows, width), F32)],
        in_specs=[anywhere] * 6,
        out_specs=[vmem] * 6,
        scratch_shapes=[pltpu.VMEM(slab, F32)] * 4
        + [
            pltpu.VMEM((rows, width), F32),
            pltpu.SMEM(weights.shape, F32),
            pltpu.VMEM((4, 2, levels, 2, width), F32),
            pltpu.VMEM((2, 2, levels, width), F32),
            pltpu.VMEM((2, 2, levels, width), F32),
            pltpu.VMEM((2, 2, width), F32),
            pltpu.VMEM((2, 2, width), F32),
            pltpu.VMEM((2, 3, levels, width), F32),
            pltpu.VMEM((2, 3, levels, width), F32),
            pltpu.VMEM((2, half, width), F32),
            pltpu.VMEM((2, along_y, half, width), F32),
            pltpu.VMEM((2, half, width), F32),
            pltpu.VMEM((2, along_x, half, width), F32),
            pltpu.VMEM((along_x, half, width), F32),
            pltpu.VMEM((2, half, width), F32),
            pltpu.VMEM((along_y, half, width), F32),
            pltpu.VMEM((2, half, width), F32),
            pltpu.VMEM((4, width), F32),
            pltpu.VMEM((levs, 4, width), F32),
            dma((6,)),
            dma((4, 2)),
            dma((3, 2)),
            dma((3, 2)),
            dma((3, along_y)),
            dma((3, along_y)),
            dma((3, along_x)),
            dma((3, along_x)),
            dma((levs,)),
            dma((levs,)),
            pltpu.SemaphoreType.REGULAR,
        ],
        compiler_params=pltpu.CompilerParams(
            collective_id=0, has_side_effects=True, vmem_limit_bytes=32 * 2**20
        ),
    )(*args)
    return pl.pallas_call(
        finish_kernel,
        name="finish",
        out_shape=[jax.ShapeDtypeStruct(slab, F32)] * 5,
        in_specs=[vmem] * 6,
        out_specs=[anywhere] * 5,
        scratch_shapes=[pltpu.VMEM(slab, F32)] * 3 + [dma((5,))],
        compiler_params=pltpu.CompilerParams(vmem_limit_bytes=16 * 2**20),
    )(*parts)


def solution(mesh):
    slab = P("lev", "lat", None)
    return jax.shard_map(
        body,
        mesh=mesh,
        in_specs=(slab,) * 4 + (P("lat", None), P()),
        out_specs=(slab,) * 5,
        check_vma=False,
    )
```

time: 19.2 us -> 18.1 us (0.943)
  the two profiles are of different devices: /device:TPU:2 before, /device:TPU:225 now
where the time goes in v3:
time: 18.1 us; the launch traced here: 17.9 us
  Pallas kernels  17.2 us (95%)
  between operations  0.64 us (4%)
    pallas_call x1, Pallas kernels, body(): pl.pallas_call(advect_kernel, name='advect', out_shape=[pltpu.VMEM(slab,...  16 us
    pallas_call x1, Pallas kernels, body(): pl.pallas_call(finish_kernel, name='finish', out_shape=[jax.ShapeDtypeStr...  1.2 us

profile of v3, /device:TPU:225, one launch (start us, length us, event | category | flops | bytes accessed | tf_op | source)
XLA Modules:
  0.0 17.9 jit_solution(11721742738850167933)
XLA Ops:
  0.6 16.0 %advect.1 = (f32[8,16,576]{2,1,0:T(8,128)S(1)}, f32[8,16,576]{2,1,0:T(8,128)S(1)}, f32[8,16,576]{2,1,0:T(8,128)S(1)}, f32[8,16,576]{2,1,0:T(8,128)S(1)}, f32[8,1...) custom-call(f32[8,16,576]{2,1,0:T(8,128)} %u_hbm.1, f32[8,16,576]{2,1,0:T(8,128)} %v_hbm.1, f32[8,16,576]{2,1,0:T(8,128)} %t_hbm.1, ...), custom_call_target="tpu_custom_call" | custom-call | tf_op jit(solution)/shard_map/advect/pallas_call | solution.py:551
  16.7 1.2 %finish.1 = (f32[8,16,576]{2,1,0:T(8,128)}, f32[8,16,576]{2,1,0:T(8,128)}, f32[8,16,576]{2,1,0:T(8,128)}, f32[8,16,576]{2,1,0:T(8,128)}, f32[8,16,576]{2,1,0:T(8,128)}) custom-call(f32[8,16,576]{2,1,0:T(8,128)S(1)} %get-tuple-element.11.t_in, f32[8,16,576]{2,1,0:T(8,128)S(1)} %get-tuple-element.12.q_in, f32[8,16,576]{2,1,0:T(8,128)S(1)} %get-tuple-element.13.u_in, ...), custom_call_target="tpu_custom_call" | custom-call | tf_op jit(solution)/shard_map/finish/pallas_call | solution.py:594

commit v4 on v3

--- a/solution.py
+++ b/solution.py
@@ -56,16 +56,18 @@
 def advect_kernel(
     u_hbm, v_hbm, t_hbm, q_hbm, g_hbm, w_hbm,
     t_out, q_out, u_out, v_out, c_out, b_out,
-    u_ref, v_ref, t_ref, q_ref, g_ref, w_ref, edge_rows,
+    whole_ref, g_ref, w_ref, edge_rows,
     first_send, first_recv, rows_send, rows_recv, rest_send, rest_recv,
     sum_send, meet_y, total_send, far_x, meet_x, pair_send, far_y, hold_ref,
     late_send, late_recv,
-    in_sem, edge_sem, halo_ssem, halo_rsem, y_ssem, y_rsem, x_ssem, x_rsem, late_ssem, late_rsem, ready,
+    in_sem, halo_ssem, halo_rsem, sum_ssem, sum_rsem, late_ssem, late_rsem, ready,
 ):
     lat, lev = lax.axis_index("lat"), lax.axis_index("lev")
     lats, levs = lax.axis_size("lat"), lax.axis_size("lev")
     along_y = meet_y.shape[1]
+    groups = levs // along_y
     x, y = lev // along_y, lev % along_y
+    v_ref, t_ref, q_ref, u_ref = [whole_ref.at[kind] for kind in range(4)]
     levels, rows, width = t_ref.shape
     half = rows // 2
     circle_sum = rows * lats
@@ -97,18 +99,20 @@
 
     edge_loads = [
         pltpu.make_async_copy(
-            source.at[:, pl.ds(side * (rows - 2), 2), :], edge_rows.at[kind, side], edge_sem.at[kind, side]
+            source.at[:, pl.ds(side * (rows - 2), 2), :], edge_rows.at[kind, side], in_sem.at[2]
         )
         for kind, source in enumerate([v_hbm, t_hbm, q_hbm, u_hbm])
         for side in (0, 1)
     ]
-    loads = [
-        pltpu.make_async_copy(source, target, in_sem.at[n])
-        for n, (source, target) in enumerate(
-            [(w_hbm, w_ref), (g_hbm, g_ref), (t_hbm, t_ref), (q_hbm, q_ref), (u_hbm, u_ref), (v_hbm, v_ref)]
-        )
+    small_loads = [
+        pltpu.make_async_copy(w_hbm, w_ref, in_sem.at[0]),
+        pltpu.make_async_copy(g_hbm, g_ref, in_sem.at[1]),
     ]
-    for load in edge_loads + loads[:2]:
+    whole_loads = [
+        pltpu.make_async_copy(source, whole_ref.at[kind], in_sem.at[3])
+        for kind, source in enumerate([v_hbm, t_hbm, q_hbm, u_hbm])
+    ]
+    for load in edge_loads + small_loads:
         load.start()
 
     band = (lat * rows + lax.broadcasted_iota(jnp.int32, (rows, 128), 0)).astype(F32)
@@ -160,9 +164,8 @@
         pl.when(has_south)(halos[kind][1].wait_recv)
         pl.when(has_north)(halos[kind][0].wait_recv)
 
-    for load in edge_loads:
-        load.wait()
-    for load in loads[2:]:
+    pltpu.make_async_copy(edge_rows, edge_rows, in_sem.at[2]).wait()
+    for load in whole_loads:
         load.start()
 
     def edge_row(kind, side, inner=False):
@@ -171,23 +174,18 @@
     for side in (0, 1):
         first_send[side, 0] = edge_row(0, side)
         first_send[side, 1] = edge_row(1, side) + MOIST_CORRECTION * edge_row(2, side)
-    pl.semaphore_wait(
-        barrier,
-        jnp.where(first, levs - 1, lev - first_band.astype(jnp.int32) + along_y - 1 - y)
-        + has_south.astype(jnp.int32)
-        + has_north.astype(jnp.int32),
-    )
-    start_halos(0)
-
-    @pl.when(first)
-    def _():
-        def answer(slab, carry):
-            pl.semaphore_signal(ready, inc=1, device_id=(lat, slab), device_id_type=MESH)
-            return carry
-
-        lax.fori_loop(1, levs, answer, 0)
-
-    for load in loads[:2]:
+    def enter():
+        pl.semaphore_wait(
+            barrier,
+            jnp.where(first, levs - 1, lev - first_band.astype(jnp.int32) + along_y - 1 - y)
+            + has_south.astype(jnp.int32)
+            + has_north.astype(jnp.int32),
+        )
+        start_halos(0)
+
+    ahead = lat % 2 == 1
+    pl.when(jnp.logical_not(ahead))(enter)
+    for load in small_loads:
         load.wait()
     level_of = lax.broadcasted_iota(jnp.int32, (levels, 128), 0)
     weights = jnp.zeros((levels, 128), F32)
@@ -220,10 +218,21 @@
         rest_send[side, 2] = part
         rows_send[side, 0:1] = jnp.sum(weights * part, axis=0, keepdims=True)
         rows_send[side, 1:2] = g_ref[row : row + 1, :]
-    start_halos(1)
-    start_halos(2)
-    for load in loads[2:]:
-        load.wait()
+
+    def start_rest():
+        start_halos(1)
+        start_halos(2)
+
+        @pl.when(first)
+        def _():
+            def answer(slab, carry):
+                pl.semaphore_signal(ready, inc=1, device_id=(lat, slab), device_id_type=MESH)
+                return carry
+
+            lax.fori_loop(1, levs, answer, 0)
+
+    pl.when(jnp.logical_not(ahead))(start_rest)
+    pltpu.make_async_copy(whole_ref, whole_ref, in_sem.at[3]).wait()
 
     def partial(k, carry):
         zonal_sum, merid_sum, own_sum = carry
@@ -255,64 +264,69 @@
     sum_send[0] = slab_sum[:half]
     sum_send[1] = slab_sum[half:]
 
-    def along(ssem, rsem, source, target, here, leg, other, slab):
+    def along(source, target, here, leg, part, slab):
         return pltpu.make_async_remote_copy(
             src_ref=source,
             dst_ref=target.at[here],
-            send_sem=ssem.at[leg, other],
-            recv_sem=rsem.at[leg, here],
+            send_sem=sum_ssem.at[leg, part],
+            recv_sem=sum_rsem.at[leg, part],
             device_id=(lat, slab),
             device_id_type=MESH,
         )
 
-    def to_y(leg, source, target, other):
-        return along(y_ssem, y_rsem, source, target, y, leg, other, x * along_y + other)
-
-    def to_x(leg, source, target, other):
-        return along(x_ssem, x_rsem, source, target, x, leg, other, other * along_y + y)
-
-    def wait_slot(target, slot, sem):
-        pltpu.make_async_copy(target.at[slot], target.at[slot], sem).wait()
+    def to_y(leg, part, source, target, other):
+        return along(source, target, y, leg, part, x * along_y + other)
+
+    def to_x(leg, part, source, target, other):
+        return along(source, target, x, leg, part, other * along_y + y)
+
+    def wait_blocks(count, blocks, sem):
+        for some in range(1, blocks.shape[0]):
+
+            @pl.when(count == some)
+            def _(some=some):
+                taken = blocks.at[pl.ds(0, some)]
+                pltpu.make_async_copy(taken, taken, sem).wait()
 
     def start(copy):
         copy.start()
 
-    def wait_send(copy):
-        copy.wait_send()
-
     steps = sorted(range(1, along_y), key=lambda step: -min(step, along_y - step))
     swapped = jnp.logical_not(first_band)
+    turned = (ahead, swapped)
 
     def meet_along_y(part, act):
         for step in steps:
             other = (y + step) % along_y
             wanted = (x > 0) | ((other < y) & ((other > 0) | swapped))
-            pl.when(wanted)(lambda other=other: act(to_y(part, sum_send.at[part], meet_y.at[part], other)))
-
-    def meet_along_x(act):
-        lax.fori_loop(0, x, lambda other, c: (act(to_x(2, sum_send.at[1], meet_x, other)), c)[1], 0)
+            pl.when(wanted)(lambda other=other: act(to_y(0, part, sum_send.at[part], meet_y.at[part], other)))
+
+    def meet_along_x(part, act):
+        lax.fori_loop(
+            0, x, lambda other, c: (act(to_x(0, part, sum_send.at[part], meet_x.at[part], other)), c)[1], 0
+        )
 
     def far_along_x(part, act):
         begin = jnp.where(first_band & (y == 0), 1, 0)
         lax.fori_loop(
-            begin, x, lambda other, c: (act(to_x(part, total_send.at[part], far_x.at[part], other)), c)[1], 0
-        )
-
-    def far_along_y(act):
+            begin, x, lambda other, c: (act(to_x(1, part, total_send.at[part], far_x.at[part], other)), c)[1], 0
+        )
+
+    def far_along_y(part, act):
         for step in steps:
             other = (y + step) % along_y
-            act(to_y(2, pair_send.at[(y + step) // along_y], far_y, other))
+            act(to_y(1, part, pair_send.at[part, (y + step) // along_y], far_y.at[part], other))
 
     def to_first(act):
         @pl.when(first_band & (x == 0) & (y > 0))
         def _():
             for part in (0, 1):
-                act(to_y(part, sum_send.at[part], meet_y.at[part], 0))
+                act(to_y(0, part, sum_send.at[part], meet_y.at[part], 0))
 
         @pl.when(first_band & (x > 0) & (y == 0))
         def _():
             for part in (0, 1):
-                act(to_x(part, total_send.at[part], far_x.at[part], 0))
+                act(to_x(1, part, total_send.at[part], far_x.at[part], 0))
 
         pl.when(first_band & (lev > 0))(lambda: act(to_lower(0)))
 
@@ -320,8 +334,8 @@
         return pltpu.make_async_remote_copy(
             src_ref=late_send,
             dst_ref=late_recv.at[lev],
-            send_sem=late_ssem.at[other],
-            recv_sem=late_rsem.at[lev],
+            send_sem=late_ssem.at[0],
+            recv_sem=late_rsem.at[0],
             device_id=(lat, other),
             device_id_type=MESH,
         )
@@ -331,9 +345,10 @@
             first_band.astype(jnp.int32), lev, lambda other, c: (act(to_lower(other)), c)[1], 0
         )
 
-    meet_along_y(0, start)
-    pl.when(first_band)(lambda: meet_along_y(1, start))
-    pl.when(swapped)(lambda: meet_along_x(start))
+    pl.when(ahead)(lambda: (enter(), start_rest(), None)[-1])
+    for part in (0, 1):
+        pl.when(jnp.logical_not(turned[part]))(lambda part=part: meet_along_y(part, start))
+        pl.when(turned[part])(lambda part=part: meet_along_x(part, start))
 
     @pl.when(lev > 0)
     def _():
@@ -348,15 +363,11 @@
         late_to_lower(start)
 
     def second_along_x(part):
+        wait_blocks(jnp.where(x > 0, along_y - 1, along_y - 1 - y), meet_y.at[part], sum_rsem.at[0, part])
         below, total_y = jnp.zeros((half, width), F32), sum_send[part]
         for step in range(1, along_y):
             other = (y + step) % along_y
             comes = (x > 0) | (other > y)
-
-            @pl.when(comes)
-            def _(other=other):
-                wait_slot(meet_y.at[part], other, y_rsem.at[part, other])
-
             came = jnp.where(comes, meet_y[part, other], 0.0)
             total_y += came
             below += jnp.where(other > y, came, 0.0)
@@ -364,20 +375,21 @@
         hold_ref[part] = below
         far_along_x(part, start)
 
-    def second_along_y():
+    def second_along_y(part):
+        wait_blocks(groups - 1 - x, meet_x.at[part], sum_rsem.at[0, part])
+
         def add(other, total):
-            wait_slot(meet_x, other, x_rsem.at[2, other])
-            return total + meet_x[other]
+            return total + meet_x[part, other]
 
         below = lax.fori_loop(x + 1, levs // along_y, add, jnp.zeros((half, width), F32))
-        hold_ref[1] = below
-        pair_send[0] = below
-        pair_send[1] = below + sum_send[1]
-        far_along_y(start)
-
-    second_along_x(0)
-    pl.when(first_band)(lambda: second_along_x(1))
-    pl.when(swapped)(second_along_y)
+        hold_ref[part] = below
+        pair_send[part, 0] = below
+        pair_send[part, 1] = below + sum_send[part]
+        far_along_y(part, start)
+
+    for part in (0, 1):
+        pl.when(jnp.logical_not(turned[part]))(lambda part=part: second_along_x(part))
+        pl.when(turned[part])(lambda part=part: second_along_y(part))
 
     @pl.when(first_band & (lev > 0))
     def _():
@@ -452,23 +464,24 @@
         v_out[:, beside_row, :] = v_out[:, beside_row, :] + across * edge
 
     def last_along_x(part):
+        wait_blocks(groups - 1 - x, far_x.at[part], sum_rsem.at[1, part])
+
         def add(other, total):
-            wait_slot(far_x.at[part], other, x_rsem.at[part, other])
             return total + far_x[part, other]
 
         hold_ref[part] = lax.fori_loop(x + 1, levs // along_y, add, hold_ref[part])
 
-    def last_along_y():
-        total = hold_ref[1]
+    def last_along_y(part):
+        wait_blocks(along_y - 1, far_y.at[part], sum_rsem.at[1, part])
+        total = hold_ref[part]
         for step in range(1, along_y):
             other = (y + step) % along_y
-            wait_slot(far_y, other, y_rsem.at[2, other])
-            total += far_y[other]
-        hold_ref[1] = total
-
-    last_along_x(0)
-    pl.when(first_band)(lambda: last_along_x(1))
-    pl.when(swapped)(last_along_y)
+            total += far_y[part, other]
+        hold_ref[part] = total
+
+    for part in (0, 1):
+        pl.when(jnp.logical_not(turned[part]))(lambda part=part: last_along_x(part))
+        pl.when(turned[part])(lambda part=part: last_along_y(part))
     total = g_ref[...] + jnp.concatenate([hold_ref[0], hold_ref[1]], axis=0)
 
     around = wrapped(total)
@@ -479,9 +492,9 @@
     b_out[2] = 0.5 * MERID_RATE * (north - south)
 
     def add_late(other, total):
-        wait_slot(late_recv, other, late_rsem.at[other])
         return total + late_recv[other]
 
+    wait_blocks(levs - 1 - lev, late_recv, late_rsem.at[0])
     edges = lax.fori_loop(lev + 1, levs, add_late, jnp.zeros(late_send.shape, F32))
     for side, exists, row, beside_row, merid_edge, sign in (
         (0, has_north, rows - 1, rows - 2, merid_north, 1.0),
@@ -501,21 +514,20 @@
     for kind in range(3):
         pl.when(has_south)(halos[kind][0].wait_send)
         pl.when(has_north)(halos[kind][1].wait_send)
-    meet_along_y(0, wait_send)
-    far_along_x(0, wait_send)
-
-    @pl.when(first_band)
-    def _():
-        meet_along_y(1, wait_send)
-        far_along_x(1, wait_send)
-
-    @pl.when(swapped)
-    def _():
-        meet_along_x(wait_send)
-        far_along_y(wait_send)
-
-    to_first(wait_send)
-    late_to_lower(wait_send)
+
+    for part in (0, 1):
+
+        @pl.when(jnp.logical_not(turned[part]))
+        def _(part=part):
+            wait_blocks(jnp.where(x > 0, along_y - 1, y), meet_y.at[part], sum_ssem.at[0, part])
+            wait_blocks(x, far_x.at[part], sum_ssem.at[1, part])
+
+        @pl.when(turned[part])
+        def _(part=part):
+            wait_blocks(x, meet_x.at[part], sum_ssem.at[0, part])
+            wait_blocks(along_y - 1, far_y.at[part], sum_ssem.at[1, part])
+
+    wait_blocks(lev, late_recv, late_ssem.at[0])
 
 
 def finish_kernel(t_in, q_in, u_in, v_in, c_in, b_in, t, q, u, v, h, u_new, v_new, h_new, sems):
@@ -554,8 +566,8 @@
         out_shape=[pltpu.VMEM(slab, F32)] * 5 + [pltpu.VMEM((3, rows, width), F32)],
         in_specs=[anywhere] * 6,
         out_specs=[vmem] * 6,
-        scratch_shapes=[pltpu.VMEM(slab, F32)] * 4
-        + [
+        scratch_shapes=[
+            pltpu.VMEM((4,) + slab, F32),
             pltpu.VMEM((rows, width), F32),
             pltpu.SMEM(weights.shape, F32),
             pltpu.VMEM((4, 2, levels, 2, width), F32),
@@ -569,22 +581,19 @@
             pltpu.VMEM((2, along_y, half, width), F32),
             pltpu.VMEM((2, half, width), F32),
             pltpu.VMEM((2, along_x, half, width), F32),
-            pltpu.VMEM((along_x, half, width), F32),
-            pltpu.VMEM((2, half, width), F32),
-            pltpu.VMEM((along_y, half, width), F32),
+            pltpu.VMEM((2, along_x, half, width), F32),
+            pltpu.VMEM((2, 2, half, width), F32),
+            pltpu.VMEM((2, along_y, half, width), F32),
             pltpu.VMEM((2, half, width), F32),
             pltpu.VMEM((4, width), F32),
             pltpu.VMEM((levs, 4, width), F32),
-            dma((6,)),
-            dma((4, 2)),
+            dma((4,)),
             dma((3, 2)),
             dma((3, 2)),
-            dma((3, along_y)),
-            dma((3, along_y)),
-            dma((3, along_x)),
-            dma((3, along_x)),
-            dma((levs,)),
-            dma((levs,)),
+            dma((2, 2)),
+            dma((2, 2)),
+            dma((1,)),
+            dma((1,)),
             pltpu.SemaphoreType.REGULAR,
         ],
         compiler_params=pltpu.CompilerParams(

time: 18.1 us -> 17 us (0.939)
  Pallas kernels: 17.2 us -> 16.2 us
    pallas_call x1, Pallas kernels: 16 us -> 15 us  [body(): pl.pallas_call(advect_kernel, name='advect', out_shape=[pltpu.VMEM(slab,...]
where the time goes in v4:
time: 17 us; the launch traced here: 16.8 us
  Pallas kernels  16.2 us (95%)
  between operations  0.64 us (4%)
    pallas_call x1, Pallas kernels, body(): pl.pallas_call(advect_kernel, name='advect', out_shape=[pltpu.VMEM(slab,...  15 us
    pallas_call x1, Pallas kernels, body(): pl.pallas_call(finish_kernel, name='finish', out_shape=[jax.ShapeDtypeStr...  1.2 us

profile of v4, /device:TPU:225, one launch (start us, length us, event | category | flops | bytes accessed | tf_op | source)
XLA Modules:
  0.0 16.8 jit_solution(6952195379948327729)
XLA Ops:
  0.6 15.0 %advect.1 = (f32[8,16,576]{2,1,0:T(8,128)S(1)}, f32[8,16,576]{2,1,0:T(8,128)S(1)}, f32[8,16,576]{2,1,0:T(8,128)S(1)}, f32[8,16,576]{2,1,0:T(8,128)S(1)}, f32[8,1...) custom-call(f32[8,16,576]{2,1,0:T(8,128)} %u_hbm.1, f32[8,16,576]{2,1,0:T(8,128)} %v_hbm.1, f32[8,16,576]{2,1,0:T(8,128)} %t_hbm.1, ...), custom_call_target="tpu_custom_call" | custom-call | tf_op jit(solution)/shard_map/advect/pallas_call | solution.py:563
  15.6 1.2 %finish.1 = (f32[8,16,576]{2,1,0:T(8,128)}, f32[8,16,576]{2,1,0:T(8,128)}, f32[8,16,576]{2,1,0:T(8,128)}, f32[8,16,576]{2,1,0:T(8,128)}, f32[8,16,576]{2,1,0:T(8,128)}) custom-call(f32[8,16,576]{2,1,0:T(8,128)S(1)} %get-tuple-element.11.t_in, f32[8,16,576]{2,1,0:T(8,128)S(1)} %get-tuple-element.12.q_in, f32[8,16,576]{2,1,0:T(8,128)S(1)} %get-tuple-element.13.u_in, ...), custom_call_target="tpu_custom_call" | custom-call | tf_op jit(solution)/shard_map/finish/pallas_call | solution.py:603

commit v5 on v4

--- a/solution.py
+++ b/solution.py
@@ -112,7 +112,7 @@
         pltpu.make_async_copy(source, whole_ref.at[kind], in_sem.at[3])
         for kind, source in enumerate([v_hbm, t_hbm, q_hbm, u_hbm])
     ]
-    for load in edge_loads + small_loads:
+    for load in edge_loads + small_loads + whole_loads:
         load.start()
 
     band = (lat * rows + lax.broadcasted_iota(jnp.int32, (rows, 128), 0)).astype(F32)
@@ -131,6 +131,12 @@
     def spread(row):
         return widen(jnp.broadcast_to(row, (levels, 128)), width)
 
+    def clear(slab, carry):
+        late_recv[slab] = jnp.zeros(late_recv.shape[1:], F32)
+        return carry
+
+    lax.fori_loop(0, lev + 1, clear, 0)
+
     for side, exists in ((0, has_north), (1, has_south)):
 
         @pl.when(jnp.logical_not(exists))
@@ -143,7 +149,7 @@
         return pltpu.make_async_remote_copy(
             src_ref=send.at[side],
             dst_ref=recv.at[side],
-            send_sem=halo_ssem.at[kind, side],
+            send_sem=halo_ssem.at[kind],
             recv_sem=halo_rsem.at[kind, side],
             device_id=(lat - 1 if side == 0 else lat + 1, lev),
             device_id_type=MESH,
@@ -160,13 +166,10 @@
         pl.when(has_south)(halos[kind][0].start)
         pl.when(has_north)(halos[kind][1].start)
 
-    def wait_halos(kind):
-        pl.when(has_south)(halos[kind][1].wait_recv)
-        pl.when(has_north)(halos[kind][0].wait_recv)
+    def wait_halos(kind, side):
+        pl.when(has_south if side == 1 else has_north)(halos[kind][side].wait_recv)
 
     pltpu.make_async_copy(edge_rows, edge_rows, in_sem.at[2]).wait()
-    for load in whole_loads:
-        load.start()
 
     def edge_row(kind, side, inner=False):
         return edge_rows[kind, side, :, side if not inner else 1 - side, :]
@@ -281,7 +284,7 @@
         return along(source, target, x, leg, part, other * along_y + y)
 
     def wait_blocks(count, blocks, sem):
-        for some in range(1, blocks.shape[0]):
+        for some in range(1, blocks.shape[0] + 1):
 
             @pl.when(count == some)
             def _(some=some):
@@ -352,9 +355,9 @@
 
     @pl.when(lev > 0)
     def _():
-        wait_halos(0)
-        wait_halos(1)
-        for side, interface in ((0, north_interface), (1, south_interface)):
+        for side, interface in ((1, south_interface), (0, north_interface)):
+            wait_halos(0, side)
+            wait_halos(1, side)
             mine = 1 - side
             wind = spread(interface * 0.25) * (first_send[mine, 0] + first_recv[side, 0])
             flux = wind * (first_send[mine, 1] + first_recv[side, 1])
@@ -438,8 +441,15 @@
         return value
 
     level_wide = lax.broadcasted_iota(jnp.int32, (levels, width), 0)
-    pl.when(lev == 0)(lambda: (wait_halos(0), wait_halos(1), None)[-1])
-    wait_halos(2)
+
+    @pl.when(lev == 0)
+    def _():
+        for side in (0, 1):
+            wait_halos(0, side)
+            wait_halos(1, side)
+
+    for side in (0, 1):
+        wait_halos(2, side)
     for side, exists, row, beside_row, interface, merid_edge, sign in (
         (0, has_north, rows - 1, rows - 2, north_interface, merid_north, 1.0),
         (1, has_south, 0, 1, south_interface, merid_south, -1.0),
@@ -491,11 +501,11 @@
     south = jnp.where(row_of == 0, 0.0, pltpu.roll(total, 1, 0))
     b_out[2] = 0.5 * MERID_RATE * (north - south)
 
-    def add_late(other, total):
-        return total + late_recv[other]
-
     wait_blocks(levs - 1 - lev, late_recv, late_rsem.at[0])
-    edges = lax.fori_loop(lev + 1, levs, add_late, jnp.zeros(late_send.shape, F32))
+    edges = [late_recv[slab] for slab in range(levs)]
+    while len(edges) > 1:
+        edges = [sum(edges[n + 1 : n + 2], edges[n]) for n in range(0, len(edges), 2)]
+    edges = edges[0]
     for side, exists, row, beside_row, merid_edge, sign in (
         (0, has_north, rows - 1, rows - 2, merid_north, 1.0),
         (1, has_south, 0, 1, merid_south, -1.0),
@@ -511,10 +521,9 @@
         b_out[2, row : row + 1] += across * jnp.where(exists, beyond, 0.0)
         b_out[2, beside_row : beside_row + 1] += across * change
 
-    for kind in range(3):
-        pl.when(has_south)(halos[kind][0].wait_send)
-        pl.when(has_north)(halos[kind][1].wait_send)
-
+    sides = has_south.astype(jnp.int32) + has_north.astype(jnp.int32)
+    for kind, send in enumerate((first_send, rows_send, rest_send)):
+        wait_blocks(sides, send, halo_ssem.at[kind])
     for part in (0, 1):
 
         @pl.when(jnp.logical_not(turned[part]))
@@ -588,7 +597,7 @@
             pltpu.VMEM((4, width), F32),
             pltpu.VMEM((levs, 4, width), F32),
             dma((4,)),
-            dma((3, 2)),
+            dma((3,)),
             dma((3, 2)),
             dma((2, 2)),
             dma((2, 2)),

time: 17 us -> 16.9 us (level)
  no operation moved by 1% of the time
where the time goes in v5:
time: 16.9 us; the launch traced here: 16.8 us
  Pallas kernels  16.1 us (95%)
  between operations  0.64 us (4%)
    pallas_call x1, Pallas kernels, body(): pl.pallas_call(advect_kernel, name='advect', out_shape=[pltpu.VMEM(slab,...  14.9 us
    pallas_call x1, Pallas kernels, body(): pl.pallas_call(finish_kernel, name='finish', out_shape=[jax.ShapeDtypeStr...  1.2 us

profile of v5, /device:TPU:225, one launch (start us, length us, event | category | flops | bytes accessed | tf_op | source)
XLA Modules:
  0.0 16.8 jit_solution(14482185945581400516)
XLA Ops:
  0.6 14.9 %advect.1 = (f32[8,16,576]{2,1,0:T(8,128)S(1)}, f32[8,16,576]{2,1,0:T(8,128)S(1)}, f32[8,16,576]{2,1,0:T(8,128)S(1)}, f32[8,16,576]{2,1,0:T(8,128)S(1)}, f32[8,1...) custom-call(f32[8,16,576]{2,1,0:T(8,128)} %u_hbm.1, f32[8,16,576]{2,1,0:T(8,128)} %v_hbm.1, f32[8,16,576]{2,1,0:T(8,128)} %t_hbm.1, ...), custom_call_target="tpu_custom_call" | custom-call | tf_op jit(solution)/shard_map/advect/pallas_call | solution.py:572
  15.6 1.2 %finish.1 = (f32[8,16,576]{2,1,0:T(8,128)}, f32[8,16,576]{2,1,0:T(8,128)}, f32[8,16,576]{2,1,0:T(8,128)}, f32[8,16,576]{2,1,0:T(8,128)}, f32[8,16,576]{2,1,0:T(8,128)}) custom-call(f32[8,16,576]{2,1,0:T(8,128)S(1)} %get-tuple-element.11.t_in, f32[8,16,576]{2,1,0:T(8,128)S(1)} %get-tuple-element.12.q_in, f32[8,16,576]{2,1,0:T(8,128)S(1)} %get-tuple-element.13.u_in, ...), custom_call_target="tpu_custom_call" | custom-call | tf_op jit(solution)/shard_map/finish/pallas_call | solution.py:612

commit v6 on v5

--- a/solution.py
+++ b/solution.py
@@ -112,7 +112,7 @@
         pltpu.make_async_copy(source, whole_ref.at[kind], in_sem.at[3])
         for kind, source in enumerate([v_hbm, t_hbm, q_hbm, u_hbm])
     ]
-    for load in edge_loads + small_loads + whole_loads:
+    for load in edge_loads + small_loads:
         load.start()
 
     band = (lat * rows + lax.broadcasted_iota(jnp.int32, (rows, 128), 0)).astype(F32)
@@ -170,6 +170,8 @@
         pl.when(has_south if side == 1 else has_north)(halos[kind][side].wait_recv)
 
     pltpu.make_async_copy(edge_rows, edge_rows, in_sem.at[2]).wait()
+    for load in whole_loads:
+        load.start()
 
     def edge_row(kind, side, inner=False):
         return edge_rows[kind, side, :, side if not inner else 1 - side, :]

time: 16.9 us -> 17 us (level)
  no operation moved by 1% of the time
where the time goes in v6:
time: 17 us; the launch traced here: 16.8 us
  Pallas kernels  16.1 us (95%)
  between operations  0.64 us (4%)
    pallas_call x1, Pallas kernels, body(): pl.pallas_call(advect_kernel, name='advect', out_shape=[pltpu.VMEM(slab,...  14.9 us
    pallas_call x1, Pallas kernels, body(): pl.pallas_call(finish_kernel, name='finish', out_shape=[jax.ShapeDtypeStr...  1.2 us

profile of v6, /device:TPU:225, one launch (start us, length us, event | category | flops | bytes accessed | tf_op | source)
XLA Modules:
  0.0 16.8 jit_solution(7672180312754889001)
XLA Ops:
  0.6 14.9 %advect.1 = (f32[8,16,576]{2,1,0:T(8,128)S(1)}, f32[8,16,576]{2,1,0:T(8,128)S(1)}, f32[8,16,576]{2,1,0:T(8,128)S(1)}, f32[8,16,576]{2,1,0:T(8,128)S(1)}, f32[8,1...) custom-call(f32[8,16,576]{2,1,0:T(8,128)} %u_hbm.1, f32[8,16,576]{2,1,0:T(8,128)} %v_hbm.1, f32[8,16,576]{2,1,0:T(8,128)} %t_hbm.1, ...), custom_call_target="tpu_custom_call" | custom-call | tf_op jit(solution)/shard_map/advect/pallas_call | solution.py:574
  15.6 1.2 %finish.1 = (f32[8,16,576]{2,1,0:T(8,128)}, f32[8,16,576]{2,1,0:T(8,128)}, f32[8,16,576]{2,1,0:T(8,128)}, f32[8,16,576]{2,1,0:T(8,128)}, f32[8,16,576]{2,1,0:T(8,128)}) custom-call(f32[8,16,576]{2,1,0:T(8,128)S(1)} %get-tuple-element.11.t_in, f32[8,16,576]{2,1,0:T(8,128)S(1)} %get-tuple-element.12.q_in, f32[8,16,576]{2,1,0:T(8,128)S(1)} %get-tuple-element.13.u_in, ...), custom_call_target="tpu_custom_call" | custom-call | tf_op jit(solution)/shard_map/finish/pallas_call | solution.py:614
